TPU v7x, 256 devices: a whole 4x4x8 slice. The times are simulated.
256 devices in a mesh: seq: 128 (over y, z, x), chan: 2 (over core).
Axes of the slice: x: 4, y: 4, z: 8, core: 2. Of those that a mesh axis runs over, the one named last changes fastest.
Arguments:
- tower_input: bfloat16 [32768, 1536], P('seq', 'chan'), may hold values from -16 to 16, as said below
- dilated_weight: bfloat16 [3, 1536, 1536], P(None, None, 'chan'), may hold values from -0.09375 to 0.09375
- norm_gain: float32 [1536], replicated, may hold values from 0.5 to 1.5
- track_embed: bfloat16 [512, 1536], P('seq', 'chan'), may hold values from -16 to 16
- span_start: int32 [2048], replicated, may hold values from 0 to 32767, as said below
- span_end: int32 [2048], replicated, may hold values from 1 to 32768, as said below
- span_owner: int32 [2048], replicated, may hold values from 0 to 511, as said below
- positive: int32 [512], P('seq'), may hold values from 0 to 511, each once
Outputs:
- grad_input: float32 [32768, 1536], P('seq', 'chan')
- loss: float32 [], replicated
Inputs may be any that keep to these rules, and one draw needn't show every extreme that they name: `tower_input`: values of the bins' embeddings. Span s covers the bins span_start[s] to span_end[s] - 1; span 0 covers bin 0 alone. span_end[s] > span_start[s]; the last span covers bin 32768 - 1 alone. `span_owner`: every gene owns at least one span; spans of one gene may lie anywhere and may share bins with spans of other genes.
All inputs are finite; a program needn't handle non-finite values.
Results may differ from a plain program's by a relative error of at most 0.01.
Values may be sent and summed in bfloat16 or wider, within the bound.
A program may use at most 64 MiB of HBM per device.

v0:
```python
import jax
import jax.numpy as jnp
from jax import lax
from jax.sharding import PartitionSpec as P

DILATION_STEP = 128


epsilon = 1e-06
inverse_temp = 2.0
loss_scale = 64.0


def with_halo(cells, sides, width):
    for axis, dim in sides:
        count = lax.axis_size(axis)
        ends = count - 1
        head = lax.slice_in_dim(cells, 0, width, axis=dim)
        tail = lax.slice_in_dim(cells, cells.shape[dim] - width, cells.shape[dim], axis=dim)
        cells = jnp.concatenate(
            [
                lax.ppermute(tail, axis, [(i, (i + 1) % count) for i in range(ends)]),
                cells,
                lax.ppermute(head, axis, [((i + 1) % count, i) for i in range(ends)]),
            ],
            axis=dim,
        )
    return cells


def activate(values, gain):
    mean_sq = jnp.mean(values * values, axis=-1, keepdims=True)
    normed = values * lax.rsqrt(mean_sq + epsilon) * gain
    return jax.nn.gelu(normed)


def norm_back(values, gain, activated_gradient):
    mean_sq = jnp.mean(values * values, axis=-1, keepdims=True)
    inv_root = lax.rsqrt(mean_sq + epsilon)
    normed = values * inv_root * gain
    _, pull = jax.vjp(jax.nn.gelu, normed)
    scaled = gain * pull(activated_gradient)[0]
    inner = jnp.mean(values * scaled, axis=-1, keepdims=True)
    return inv_root * scaled - values * inv_root * inv_root * inv_root * inner


def per_device(
    tower_input, dilated_weight, norm_gain, track_embed, span_start, span_end, span_owner, positive
):
    sequence_rows = tower_input.shape[0]
    half = tower_input.shape[1]
    width = half * lax.axis_size("chan")
    genes_all = track_embed.shape[0] * lax.axis_size("seq")
    chan_start = lax.axis_index("chan") * half
    joined = lax.all_gather(tower_input, "chan", axis=1, tiled=True)
    x_full = joined.astype(jnp.float32)
    activated_rows = activate(x_full, norm_gain).astype(jnp.bfloat16)
    activated_padded = with_halo(activated_rows, (("seq", 0),), DILATION_STEP)
    convolved_output = jnp.dot(
        activated_padded[0:sequence_rows], dilated_weight[0], preferred_element_type=jnp.float32
    )
    convolved_output = convolved_output + jnp.dot(
        activated_padded[DILATION_STEP : DILATION_STEP + sequence_rows],
        dilated_weight[1],
        preferred_element_type=jnp.float32,
    )
    convolved_output = convolved_output + jnp.dot(
        activated_padded[2 * DILATION_STEP : 2 * DILATION_STEP + sequence_rows],
        dilated_weight[2],
        preferred_element_type=jnp.float32,
    )
    hidden = (tower_input.astype(jnp.float32) + convolved_output).astype(jnp.bfloat16)
    positions = lax.axis_index("seq") * sequence_rows + jnp.arange(sequence_rows, dtype=jnp.int32)
    member = (
        (span_start[:, None] <= positions[None, :]) & (positions[None, :] < span_end[:, None])
    ).astype(jnp.bfloat16)
    owner_hot = (span_owner[None, :] == jnp.arange(genes_all, dtype=jnp.int32)[:, None]).astype(
        jnp.bfloat16
    )
    counts = jnp.dot(owner_hot, member, preferred_element_type=jnp.float32).astype(jnp.bfloat16)
    partial_pool = jnp.dot(counts, hidden, preferred_element_type=jnp.float32)
    pooled = lax.psum_scatter(partial_pool, "seq", scatter_dimension=0, tiled=True)
    sum_sq = lax.psum(jnp.sum(pooled * pooled, axis=1), "chan")
    scale = lax.rsqrt(sum_sq / width + epsilon)
    unit = 1.0 / jnp.sqrt(jnp.float32(width))
    query = (pooled * scale[:, None] * unit).astype(jnp.bfloat16)
    local_genes = pooled.shape[0]
    query_full = lax.all_gather(query, "chan", axis=1, tiled=True)
    track_full = lax.all_gather(track_embed, "chan", axis=1, tiled=True)
    piece = lax.all_gather(track_full, "seq", axis=0, tiled=True)
    run_max = jnp.full((local_genes,), -1e30, jnp.float32)
    logits = inverse_temp * jnp.dot(query_full, piece.T, preferred_element_type=jnp.float32)
    columns = jnp.arange(piece.shape[0], dtype=jnp.int32)
    hits = columns[None, :] == positive[:, None]
    new_max = jnp.maximum(run_max, jnp.max(logits, axis=1))
    run_sum = jnp.sum(jnp.exp(logits - new_max[:, None]), axis=1)
    pos_logit = jnp.sum(jnp.where(hits, logits, 0.0), axis=1)
    run_max, run_sum, pos_logit = (new_max, run_sum, pos_logit)
    log_total = run_max + jnp.log(run_sum)
    piece = lax.all_gather(track_full, "seq", axis=0, tiled=True)
    logits = inverse_temp * jnp.dot(query_full, piece.T, preferred_element_type=jnp.float32)
    columns = jnp.arange(piece.shape[0], dtype=jnp.int32)
    hits = (columns[None, :] == positive[:, None]).astype(jnp.float32)
    weights = jnp.exp(logits - log_total[:, None])
    grad_logit = (loss_scale * (weights - hits)).astype(jnp.bfloat16)
    grad_full = inverse_temp * jnp.dot(grad_logit, piece, preferred_element_type=jnp.float32)
    grad_query = lax.dynamic_slice_in_dim(grad_full, chan_start, half, 1)
    per_gene = log_total - pos_logit
    loss = lax.psum(jnp.sum(per_gene), "seq") / genes_all
    inner = lax.psum(jnp.sum(grad_query * pooled, axis=1), "chan")
    grad_pooled = (
        unit * scale[:, None] * (grad_query - pooled * (inner * scale * scale / width)[:, None])
    ).astype(jnp.bfloat16)
    grad_genes = lax.all_gather(grad_pooled, "seq", axis=0, tiled=True)
    hidden_gradient = jnp.dot(counts.T, grad_genes, preferred_element_type=jnp.float32).astype(
        jnp.bfloat16
    )
    padded_gradient = with_halo(hidden_gradient, (("seq", 0),), DILATION_STEP)
    activated_gradient = jnp.dot(
        padded_gradient[2 * DILATION_STEP : 2 * DILATION_STEP + sequence_rows],
        dilated_weight[0].T,
        preferred_element_type=jnp.float32,
    )
    activated_gradient = activated_gradient + jnp.dot(
        padded_gradient[DILATION_STEP : DILATION_STEP + sequence_rows],
        dilated_weight[1].T,
        preferred_element_type=jnp.float32,
    )
    activated_gradient = activated_gradient + jnp.dot(
        padded_gradient[0:sequence_rows], dilated_weight[2].T, preferred_element_type=jnp.float32
    )
    activated_gradient = lax.psum(activated_gradient, "chan")
    grad_full_input = norm_back(x_full, norm_gain, activated_gradient)
    norm_part = lax.dynamic_slice_in_dim(grad_full_input, chan_start, half, 1)
    grad_input = hidden_gradient.astype(jnp.float32) + norm_part
    return (grad_input, loss)


def solution(mesh):
    return jax.shard_map(
        per_device,
        mesh=mesh,
        in_specs=(
            P("seq", "chan"),
            P(None, None, "chan"),
            P(),
            P("seq", "chan"),
            P(),
            P(),
            P(),
            P("seq"),
        ),
        out_specs=(P("seq", "chan"), P()),
        check_vma=False,
    )
```

profile of v0, /device:TPU:2, one launch (start us, length us, event | category | flops | bytes accessed | tf_op | source)
XLA Modules:
  0.0 1094.4 jit_solution(371002072303293192)
XLA Ops:
  7.2 2.6 all_gather.16
  10.1 1.8 convert_multiply_fusion.1
  12.8 4.2 collective-permute-start.1
  17.0 2.1 collective-permute-start
  19.1 2.4 fusion.8
  21.6 1.3 fusion.47
  22.9 3.3 collective-permute-done.1
  26.2 3.5 fusion.4
  30.2 4.2 fusion.45
  35.1 1.9 all_gather.18
  38.3 224.6 %all-reduce.6.cloned.1.call-done = f32[512,768]{1,0:T(8,128)} async-done(((f32[512,768]{1,0:T(8,128)}), f32[512,768]{1,0:T(8,128)}) %all-reduce.6.cloned.1.call-update) | async-done | bytes 1572880
  263.8 2.5 psum.28
  267.1 1.8 all_gather.17
  268.9 99.2 %all-gather.4.cloned.1.call-done = bf16[128,4,1536]{2,1,0:T(4,128)(2,1)} async-done(((bf16[1,4,1536]{2,1,0:T(4,128)(2,1)}), bf16[128,4,1536]{2,1,0:T(4,128)(2,1)}) %all-gather.4.cloned.1.call-update) | async-done | bytes 1572880 | tf_op jit(solution)/shard_map/all_gather | solution.py:100
  368.0 2.7 reshape.39
  373.5 2.5 psum.29
  376.8 342.6 %all-gather.1 = bf16[128,4,768]{2,1,0:T(4,128)(2,1)S(1)} all-gather(bf16[1,4,768]{2,1,0:T(4,128)(2,1)S(1)} %fusion.63), channel_id=1, replica_groups=mesh['seq'=128,'chan'=2] {'seq'}, dimensions={0}, use_global_device_ids=true | all-gather | bytes 792576 | tf_op jit(solution)/shard_map/all_gather | solution.py:114
  720.0 3.0 collective-permute-start.3
  723.0 6.7 collective-permute-start.2
  729.7 2.5 fusion.6
  732.2 2.5 fusion.2
  734.7 3.7 fusion.1
  738.4 343.5 %psum.31 = f32[]{:T(128)} all-reduce(f32[]{:T(128)} %get-tuple-element.4), channel_id=1, replica_groups=mesh['seq'=128,'chan'=2] {'seq'}, use_global_device_ids=true, to_apply=%region_12.13 | all-reduce | flops 1 | bytes 8 | tf_op jit(solution)/shard_map/psum | solution.py:109
  1082.5 3.0 fusion.31
  (49 shorter events, 10.1 us)
Async XLA Ops:
  7.2 2.9 copy-start.2
  7.2 255.8 %all-reduce.6.cloned.1.call-start = ((), (), s32[]{:S(2)}) async-start(), calls=%async_computation.2 | async-start | bytes 3145728
  12.8 13.4 %collective-permute-start.1 = (bf16[128,1536]{1,0:T(8,128)(2,1)}, bf16[128,1536]{1,0:T(8,128)(2,1)}, u32[]{:S(2)}, u32[]{:S(2)}) collective-permute-start(bf16[128,1536]{1,0:T(8,128)(2,1)} %get-tuple-element.11), channel_id=1, source_target_pairs={{2,0},{4,2},{6,4},{8,6},{10,8},{12,10},{14,12},{16,14},{18,16},{20... | collective-permute-start | bytes 1179656 | tf_op jit(solution)/shard_map/ppermute | solution.py:24
  17.0 4.6 copy-start.5
  17.0 4.6 copy-start.6
  17.0 4.6 copy-start.7
  17.0 13.1 %collective-permute-start = (bf16[128,1536]{1,0:T(8,128)(2,1)}, bf16[128,1536]{1,0:T(8,128)(2,1)S(1)}, u32[]{:S(2)}, u32[]{:S(2)}) collective-permute-start(bf16[128,1536]{1,0:T(8,128)(2,1)} %get-tuple-element.10), channel_id=1, source_target_pairs={{0,2},{2,4},{4,6},{6,8},{8,10},{10,12},{12,14},{14,16},{16,18},{18... | collective-permute-start | bytes 1179656 | tf_op jit(solution)/shard_map/ppermute | solution.py:22
  22.9 7.3 copy-start.1
  34.4 0.7 copy-start.3
  34.4 2.7 copy-start.8
  34.4 333.6 %all-gather.4.cloned.1.call-start = ((), (), s32[]{:S(2)}) async-start(), calls=%async_computation.1 | async-start | bytes 1585152 | tf_op jit(solution)/shard_map/all_gather | solution.py:100
  37.0 1045.5 %all-reduce.4.cloned.1.call-start = ((), (), s32[]{:S(2)}) async-start(), calls=%async_computation | async-start | bytes 3145728 | tf_op jit(solution)/shard_map/psum | solution.py:132
  370.8 0.7 copy-start.4
  720.0 12.2 %collective-permute-start.3 = (bf16[128,768]{1,0:T(8,128)(2,1)S(1)}, bf16[128,768]{1,0:T(8,128)(2,1)S(1)}, u32[]{:S(2)}, u32[]{:S(2)}) collective-permute-start(bf16[128,768]{1,0:T(8,128)(2,1)S(1)} %get-tuple-element.13), channel_id=1, source_target_pairs={{0,2},{2,4},{4,6},{6,8},{8,10},{10,12},{12,14},{14,16},{16,18},{18... | collective-permute-start | bytes 589832 | tf_op jit(solution)/shard_map/ppermute | solution.py:22
  723.0 11.7 %collective-permute-start.2 = (bf16[128,768]{1,0:T(8,128)(2,1)S(1)}, bf16[128,768]{1,0:T(8,128)(2,1)S(1)}, u32[]{:S(2)}, u32[]{:S(2)}) collective-permute-start(bf16[128,768]{1,0:T(8,128)(2,1)S(1)} %get-tuple-element.12), channel_id=1, source_target_pairs={{2,0},{4,2},{6,4},{8,6},{10,8},{12,10},{14,12},{16,14},{18,16},{20... | collective-permute-start | bytes 589832 | tf_op jit(solution)/shard_map/ppermute | solution.py:24
  1082.5 3.0 copy-start
Sparse Core Ops, SparseCore 0:
  34.5 228.3 all-reduce.5
  266.9 101.1 all-gather.3
  738.5 23.8 all-reduce.3
where the time goes:
time: 1100 us; the launch traced here: 1090 us
  blocking collectives  697 us (63%)
  waiting for transfers between devices  328 us (30%)
  matrix products  21.3 us (2%)
  between operations  16.4 us (1%)
  starting transfers between devices  16.1 us (1%)
    psum x1, blocking collectives, per_device(): loss = lax.psum(jnp.sum(per_gene), 'seq') / genes_all  343 us
    all_gather x1, blocking collectives, per_device(): grad_genes = lax.all_gather(grad_pooled, 'seq', axis=0, tiled=True)  343 us
    unnamed x4, waiting for transfers between devices  225 us
    all_gather x1, waiting for transfers between devices, per_device(): piece = lax.all_gather(track_full, 'seq', axis=0, tiled=True)  99.2 us
  transfers between devices with their start and end apart: 7, of which 4 were waited for; matrix products, arithmetic and copies ran while one was open for 1% of the time, Pallas kernels for 0%

commit v1 on v0

v1 whole, which is shorter than its diff:
```python
import functools

import jax
import jax.numpy as jnp
from jax import lax
from jax.experimental import pallas as pl
from jax.experimental.pallas import tpu as pltpu
from jax.sharding import PartitionSpec as P

STEP = 128
TAPS = 3
EPS = 1e-06
INV_TEMP = 2.0
LOSS_SCALE = 64.0
MESH = pl.DeviceIdType.MESH
F32 = jnp.float32
BF16 = jnp.bfloat16
ROWS = 32
PIECES = 2
GELU_A = 0.7978845608028654
GELU_B = 0.044715


def first_order(value, dims, genes_each):
    ny, nz, nx = dims
    place = lax.rem(value, genes_each)
    owner = lax.div(value, genes_each)
    x = lax.rem(owner, nx)
    z = lax.rem(lax.div(owner, nx), nz)
    y = lax.div(owner, nx * nz)
    return ((y * nx + x) * nz + z) * genes_each + place


def second_from_first(row, dims, genes_each):
    ny, nz, nx = dims
    place = lax.rem(row, genes_each)
    z = lax.rem(lax.div(row, genes_each), nz)
    plane = lax.div(row, genes_each * nz)
    return (z * (ny * nx) + plane) * genes_each + place


def dot_nt(a, b):
    return lax.dot_general(a, b, (((1,), (1,)), ((), ())), preferred_element_type=F32)


def dot_nn(a, b):
    return jnp.dot(a, b, preferred_element_type=F32)


def phases(dims):
    ny, nz, nx = dims
    planes = ny * nx
    sizes = (
        ("core", 1),
        ("next", PIECES),
        ("prev", PIECES),
        ("left", PIECES),
        ("right", PIECES),
        ("mid", 1),
        ("last", 2),
        ("track_a1", nz),
        ("track_a2", planes),
        ("track_b1", planes),
        ("track_b2", nz),
        ("pool_b1", nz),
        ("pool_a1", 2 * planes),
        ("pool_a2", nz),
        ("pool_b2", planes),
        ("grad_a1", nz),
        ("grad_a2", planes),
        ("grad_b1", planes),
        ("grad_b2", nz),
        ("loss", planes),
    )
    at, total = {}, 0
    for name, size in sizes:
        at[name] = total
        total += size
    return at, total


def kernel(
    dims,
    stop,
    x_hbm,
    w_hbm,
    gain_hbm,
    track_hbm,
    start_hbm,
    end_hbm,
    owner_hbm,
    positive_hbm,
    out_v,
    loss_ref,
    gain,
    track,
    start,
    end,
    owner,
    positive,
    xp,
    w,
    act,
    fac,
    xq,
    own_hot,
    member,
    counts,
    counts_t,
    counts_b,
    counts_tb,
    perm,
    perm_t,
    acc,
    hid,
    send_a,
    recv_a,
    send_b,
    recv_b,
    tmp_a,
    tmp_b,
    send_a2,
    recv_a2,
    send_b2,
    recv_b2,
    track_a1,
    track_b1,
    trk_a,
    trk_raw,
    trk_b,
    mid_out,
    mid_in,
    grad_a1,
    grad_b1,
    grad_a,
    grad_b,
    loss_out,
    loss_in,
    hg,
    ga_mine,
    ga_send,
    ga_recv,
    load_sem,
    send_sem,
    recv_sem,
):
    ny, nz, nx = dims
    nseq = ny * nz * nx
    planes = ny * nx
    rows, half = out_v.shape
    padded = rows + 2 * STEP
    width = 2 * half
    gl = track.shape[0]
    genes = gl * nseq
    group_a = gl * nz
    group_b = gl * planes
    cols = half // 3
    wide_a = 2 * cols
    first_sem, _ = phases(dims)
    me = lax.axis_index("seq")
    c = lax.axis_index("chan")
    oc = 1 - c
    x = lax.rem(me, nx)
    z = lax.rem(lax.div(me, nx), nz)
    y = lax.div(me, nx * nz)
    p = y * nx + x
    nxt = lax.rem(me + 1, nseq)
    prv = lax.rem(me + nseq - 1, nseq)

    def plane_at(q):
        return (lax.div(q, nx) * nz + z) * nx + lax.rem(q, nx)

    def plane_to(k):
        return lax.rem(p + k, planes)

    def plane_from(k):
        return lax.rem(p + planes - k, planes)

    def z_at(q):
        return (y * nz + q) * nx + x

    def z_to(k):
        return lax.rem(z + k, nz)

    def z_from(k):
        return lax.rem(z + nz - k, nz)

    def rows_a(q):
        return pl.ds(pl.multiple_of(q * group_a, group_a), group_a)

    def rows_b(q):
        return pl.ds(pl.multiple_of(q * group_b, group_b), group_b)

    def loop(lo, hi, body):
        def step(i, carry):
            body(i)
            return carry

        lax.fori_loop(lo, hi, step, 0)

    def remote(src, dst, name, k, seq, chan):
        return pltpu.make_async_remote_copy(
            src_ref=src,
            dst_ref=dst,
            send_sem=send_sem.at[first_sem[name] + k],
            recv_sem=recv_sem.at[first_sem[name] + k],
            device_id=(seq, chan),
            device_id_type=MESH,
        )

    barrier = pltpu.get_barrier_semaphore()

    def greet(seq, chan):
        pl.semaphore_signal(barrier, inc=1, device_id=(seq, chan), device_id_type=MESH)

    loop(1, nz, lambda k: greet(z_at(z_to(k)), c))
    loop(1, planes, lambda k: greet(plane_at(plane_to(k)), c))
    greet(nxt, c)
    greet(prv, c)
    greet(me, oc)

    mid_rows = pl.ds(STEP, rows)
    smalls = [
        pltpu.make_async_copy(src, dst, load_sem.at[4 + i])
        for i, (src, dst) in enumerate(
            (
                (track_hbm, track),
                (start_hbm, start),
                (end_hbm, end),
                (owner_hbm, owner),
                (gain_hbm, gain),
                (positive_hbm, positive),
            )
        )
    ]
    load_x = pltpu.make_async_copy(x_hbm, xp.at[c, mid_rows], load_sem.at[0])
    load_w = [
        pltpu.make_async_copy(w_hbm.at[k], w.at[k], load_sem.at[1 + k]) for k in range(TAPS)
    ]
    for copy in smalls:
        copy.start()
    load_x.start()
    for copy in smalls:
        copy.wait()
    own_track = track[...].astype(F32)
    track_a1[z] = own_track[:, 0:wide_a]
    track_b1[p] = own_track[:, wide_a:half]
    load_x.wait()
    pl.semaphore_wait(barrier, 3 + planes - 1 + nz - 1)

    piece = STEP // PIECES

    def to_next(i):
        src = pl.ds(rows + i * piece, piece)
        return remote(xp.at[c, src], xp.at[c, pl.ds(i * piece, piece)], "next", i, nxt, c)

    def to_prev(i):
        src = pl.ds(STEP + i * piece, piece)
        dst = pl.ds(STEP + rows + i * piece, piece)
        return remote(xp.at[c, src], xp.at[c, dst], "prev", i, prv, c)

    def core(side):
        return remote(xp.at[side, mid_rows], xp.at[side, mid_rows], "core", 0, me, oc)

    def left(side, i):
        some = pl.ds(i * piece, piece)
        return remote(xp.at[side, some], xp.at[side, some], "left", i, me, oc)

    def right(side, i):
        some = pl.ds(STEP + rows + i * piece, piece)
        return remote(xp.at[side, some], xp.at[side, some], "right", i, me, oc)

    for i in range(PIECES):
        to_next(i).start()
        to_prev(i).start()
    core(c).start()

    def gather_a1(buf, name, k, slot):
        return remote(buf.at[z], buf.at[slot], name, k, z_at(z_to(k)), c)

    def gather_b1(buf, name, k, slot):
        return remote(buf.at[p], buf.at[slot], name, k, plane_at(plane_to(k)), c)

    def gather_a2(buf, name, k, q):
        return remote(buf.at[rows_a(p)], buf.at[rows_a(q)], name, k, plane_at(plane_to(k)), c)

    def gather_b2(buf, name, k, q):
        return remote(buf.at[rows_b(z)], buf.at[rows_b(q)], name, k, z_at(z_to(k)), c)

    loop(1, nz, lambda k: gather_a1(track_a1, "track_a1", k, z).start())
    loop(1, planes, lambda k: gather_b1(track_b1, "track_b1", k, p).start())
    for copy in load_w:
        copy.start()

    first = start[...]
    last = end[...]
    slot_of = first_order(owner[...], dims, gl)
    spans = first.shape[1]
    base = me * rows - STEP

    def member_rows(i):
        at = pl.multiple_of(i * ROWS, ROWS)
        bins = base + at + lax.broadcasted_iota(jnp.int32, (ROWS, spans), 0)
        inside = (first <= bins) & (bins < last)
        member[pl.ds(at, ROWS), :] = jnp.where(inside, 1.0, 0.0).astype(BF16)

    def owner_rows(i):
        at = pl.multiple_of(i * ROWS, ROWS)
        gene = at + lax.broadcasted_iota(jnp.int32, (ROWS, spans), 0)
        own_hot[pl.ds(at, ROWS), :] = jnp.where(slot_of == gene, 1.0, 0.0).astype(BF16)

    def perm_rows(i):
        at = pl.multiple_of(i * ROWS, ROWS)
        down = at + lax.broadcasted_iota(jnp.int32, (ROWS, genes), 0)
        across = lax.broadcasted_iota(jnp.int32, (1, genes), 1)
        moved = second_from_first(at + lax.broadcasted_iota(jnp.int32, (ROWS, 1), 0), dims, gl)
        some = pl.ds(at, ROWS)
        perm[some, :] = jnp.where(across == moved, 1.0, 0.0).astype(BF16)
        across = second_from_first(across, dims, gl)
        perm_t[some, :] = jnp.where(across == down, 1.0, 0.0).astype(BF16)

    loop(0, genes // ROWS, owner_rows)
    loop(0, padded // ROWS, member_rows)

    def normed_rows(at):
        some = pl.ds(at, ROWS)
        x0 = xp[0, some, :].astype(F32)
        x1 = xp[1, some, :].astype(F32)
        total = jnp.sum(x0 * x0, axis=1, keepdims=True) + jnp.sum(x1 * x1, axis=1, keepdims=True)
        root = lax.rsqrt(total / width + EPS)
        return (x0, x1), root

    def gain_of(h):
        return gain[h * half : (h + 1) * half].reshape(1, half)

    def gelu(n):
        return 0.5 * n * (1.0 + jnp.tanh(GELU_A * (n + GELU_B * n * n * n)))

    def gelu_slope(n):
        t = jnp.tanh(GELU_A * (n + GELU_B * n * n * n))
        return 0.5 * (1.0 + t) + 0.5 * n * (1.0 - t * t) * (
            GELU_A * (1.0 + 3.0 * GELU_B * n * n)
        )

    def activate(lo, count, keep):
        def body(i):
            at = pl.multiple_of(lo + i * ROWS, ROWS)
            xs, root = normed_rows(at)
            for h in range(2):
                act[h, pl.ds(at, ROWS), :] = (gelu(xs[h] * root * gain_of(h)) * keep).astype(BF16)

        loop(0, count // ROWS, body)

    core(oc).wait_recv()
    activate(STEP, rows, 1.0)

    for copy in load_w:
        copy.wait()

    def tap(lo, count, k, some):
        return dot_nn(act[0, lo : lo + count, :], w[k, 0:half, some]) + dot_nn(
            act[1, lo : lo + count, :], w[k, half:width, some]
        )

    def centre_cols(i):
        some = pl.ds(pl.multiple_of(i * cols, cols), cols)
        acc[:, some] = xp[c, mid_rows, some].astype(F32) + tap(STEP, rows, 1, some)
        acc[0:STEP, some] += tap(rows, STEP, 2, some)
        acc[STEP:rows, some] += tap(STEP, STEP, 0, some)

    loop(0, half // cols, centre_cols)

    def gather_turn(a1, b1, a2, b2, name):
        def a_wait(k):
            gather_a1(a1, name + "_a1", k, z_from(k)).wait_recv()

        loop(1, nz, a_wait)
        for i in range(nz):
            tmp_a[i * gl : (i + 1) * gl, :] = a1[i, :, 0:wide_a]
        a2[rows_a(p), :] = tmp_a[...].astype(BF16)
        loop(1, planes, lambda k: gather_a2(a2, name + "_a2", k, p).start())

        def b_wait(k):
            gather_b1(b1, name + "_b1", k, plane_from(k)).wait_recv()

        loop(1, planes, b_wait)
        for i in range(planes):
            tmp_b[i * gl : (i + 1) * gl, :] = b1[i]
        b2[rows_b(z), :] = tmp_b[...].astype(BF16)
        loop(1, nz, lambda k: gather_b2(b2, name + "_b2", k, z).start())

    def gather_end_a(a2, name):
        def a_wait(k):
            gather_a2(a2, name + "_a2", k, plane_from(k)).wait_recv()

        loop(1, planes, a_wait)

    def gather_end_b(b2, name):
        def b_wait(k):
            gather_b2(b2, name + "_b2", k, z_from(k)).wait_recv()

        loop(1, nz, b_wait)

    gather_turn(track_a1, track_b1, trk_a, trk_raw, "track")

    tile = min(256, genes)

    def count_rows(i):
        some = pl.ds(pl.multiple_of(i * tile, tile), tile)
        counts[some, :] = dot_nt(own_hot[some, :], member[mid_rows, :]).astype(BF16)

    keep_left = jnp.where(me > 0, 1.0, 0.0)
    keep_right = jnp.where(me < nseq - 1, 1.0, 0.0)
    for i in range(PIECES):
        to_next(i).wait_recv()
        left(c, i).start()
        to_prev(i).wait_recv()
        right(c, i).start()
        if i == 0:
            loop(0, genes // tile, count_rows)
            loop(0, genes // ROWS, perm_rows)
        else:
            counts_b[...] = dot_nn(perm_t[...], counts[...]).astype(BF16)
        left(oc, i).wait_recv()
        activate(i * piece, piece, keep_left)
        right(oc, i).wait_recv()
        activate(STEP + rows + i * piece, piece, keep_right)

    def hidden_cols(i):
        some = slice(i * cols, (i + 1) * cols)
        hid[0:STEP, some] = (acc[0:STEP, some] + tap(0, STEP, 0, some)).astype(BF16)
        hid[STEP:rows, some] = (acc[STEP:rows, some] + tap(STEP + rows, STEP, 2, some)).astype(BF16)
        return hid[:, some]

    def pool_b1(k):
        q = z_to(k)
        return remote(send_b.at[rows_b(q)], recv_b.at[k], "pool_b1", k, z_at(q), c)

    def pool_a1(i, k):
        q = plane_to(k)
        return remote(
            send_a.at[i, rows_a(q)],
            recv_a.at[i, k],
            "pool_a1",
            i * planes + k,
            plane_at(q),
            c,
        )

    send_b[...] = dot_nn(counts_b[...], hidden_cols(2)).astype(BF16)
    loop(1, nz, lambda k: pool_b1(k).start())
    for i in range(2):
        send_a[i] = dot_nn(counts[...], hidden_cols(i)).astype(BF16)
        loop(1, planes, lambda k: pool_a1(i, k).start())

    def factor_rows(i):
        at = pl.multiple_of(i * ROWS, ROWS)
        some = pl.ds(at, ROWS)
        xs, root = normed_rows(STEP + at)
        for h in range(2):
            g = gain_of(h)
            fac[h, some, :] = gelu_slope(xs[h] * root * g) * (root * g)
        xq[some, :] = jnp.where(c == 0, xs[0], xs[1]) * (root * root / width)

    loop(0, rows // ROWS, factor_rows)

    def pool_b2(k):
        q = plane_to(k)
        return remote(send_b2.at[q], recv_b2.at[k], "pool_b2", k, plane_at(q), c)

    def pool_a2(k):
        q = z_to(k)
        return remote(send_a2.at[q], recv_a2.at[k], "pool_a2", k, z_at(q), c)

    def sum_b1(k, total):
        pool_b1(k).wait_recv()
        return total + recv_b[k].astype(F32)

    tmp_b[...] = lax.fori_loop(1, nz, sum_b1, send_b[rows_b(z), :].astype(F32))
    for i in range(planes):
        send_b2[i] = tmp_b[i * gl : (i + 1) * gl, :]
    loop(1, planes, lambda k: pool_b2(k).start())

    for i in range(2):

        def sum_a1(k, total):
            pool_a1(i, k).wait_recv()
            return total + recv_a[i, k].astype(F32)

        tmp_a[:, i * cols : (i + 1) * cols] = lax.fori_loop(
            1, planes, sum_a1, send_a[i, rows_a(p), :].astype(F32)
        )
    for i in range(nz):
        send_a2[i] = tmp_a[i * gl : (i + 1) * gl, :]
    loop(1, nz, lambda k: pool_a2(k).start())

    def count_cols(i):
        some = pl.ds(pl.multiple_of(i * STEP, STEP), STEP)
        counts_t[some, :] = dot_nt(member[some, :], own_hot[...]).astype(BF16)
        counts_tb[some, :] = dot_nn(counts_t[some, :], perm[...]).astype(BF16)

    loop(0, padded // STEP, count_cols)
    gather_end_a(trk_a, "track")
    gather_end_b(trk_raw, "track")
    trk_b[...] = dot_nn(perm[...], trk_raw[...]).astype(BF16)

    def sum_b2(k, total):
        pool_b2(k).wait_recv()
        return total + recv_b2[k]

    mine_b = lax.fori_loop(1, planes, sum_b2, send_b2[p])

    def sum_a2(k, total):
        pool_a2(k).wait_recv()
        return total + recv_a2[k]

    mine_a = lax.fori_loop(1, nz, sum_a2, send_a2[z])

    raw_part = dot_nt(mine_a.astype(BF16), trk_a[...]) + dot_nt(mine_b.astype(BF16), trk_b[...])
    sq_part = jnp.sum(mine_a * mine_a, axis=1, keepdims=True) + jnp.sum(
        mine_b * mine_b, axis=1, keepdims=True
    )
    mid_out[:, 0:genes] = raw_part
    mid_out[:, genes : genes + 128] = jnp.broadcast_to(sq_part, (gl, 128))
    mid = remote(mid_out, mid_in, "mid", 0, me, oc)
    mid.start()
    mid.wait_recv()
    both = mid_out[...] + mid_in[...]
    raw = both[:, 0:genes]
    scale = lax.rsqrt(both[:, genes : genes + 1] / width + EPS)
    unit = float(width) ** -0.5
    logits = raw * (scale * (INV_TEMP * unit))
    top = jnp.max(logits, axis=1, keepdims=True)
    log_total = top + jnp.log(jnp.sum(jnp.exp(logits - top), axis=1, keepdims=True))
    place = lax.broadcasted_iota(jnp.int32, (gl, genes), 0)
    want = jnp.zeros((gl, genes), jnp.int32)
    for i in range(gl):
        want = jnp.where(place == i, first_order(positive[i], dims, gl), want)
    hits = lax.broadcasted_iota(jnp.int32, (gl, genes), 1) == want
    weights = jnp.exp(logits - log_total)
    grad_logit = (LOSS_SCALE * (weights - jnp.where(hits, 1.0, 0.0))).astype(BF16)
    inner = INV_TEMP * jnp.sum(grad_logit.astype(F32) * raw, axis=1, keepdims=True)
    back = inner * scale * scale / width
    outer = unit * scale
    grad_b1[p] = outer * (INV_TEMP * dot_nn(grad_logit, trk_b[...]) - mine_b * back)
    loop(1, planes, lambda k: gather_b1(grad_b1, "grad_b1", k, p).start())
    per_gene = log_total - jnp.sum(jnp.where(hits, logits, 0.0), axis=1, keepdims=True)
    grad_a1[z, :, 0:wide_a] = outer * (INV_TEMP * dot_nn(grad_logit, trk_a[...]) - mine_a * back)
    grad_a1[z, :, wide_a : wide_a + 128] = jnp.broadcast_to(per_gene, (gl, 128))
    loop(1, nz, lambda k: gather_a1(grad_a1, "grad_a1", k, z).start())

    gather_turn(grad_a1, grad_b1, grad_a, grad_b, "grad")
    part = jnp.zeros((1, 128), F32)
    for i in range(nz):
        part = part + jnp.sum(grad_a1[i, :, wide_a : wide_a + 128], axis=0, keepdims=True)
    loss_out[...] = jnp.broadcast_to(part, (8, 128))
    loss_in[p] = loss_out[...]

    def loss_copy(k, q):
        return remote(loss_out, loss_in.at[q], "loss", k, plane_at(plane_to(k)), c)

    loop(1, planes, lambda k: loss_copy(k, p).start())

    gather_end_b(grad_b, "grad")

    def hidden_grad_b(i):
        some = pl.ds(pl.multiple_of(i * STEP, STEP), STEP)
        hg[some, wide_a:half] = dot_nn(counts_tb[some, :], grad_b[...]).astype(BF16)

    loop(0, padded // STEP, hidden_grad_b)
    gather_end_a(grad_a, "grad")

    def hidden_grad_a(i):
        some = pl.ds(pl.multiple_of(i * STEP, STEP), STEP)
        hg[some, 0:wide_a] = dot_nn(counts_t[some, :], grad_a[...]).astype(BF16)

    loop(0, padded // STEP, hidden_grad_a)

    def activ_grad(h):
        def body(i):
            at = pl.multiple_of(i * cols, cols)
            wide = pl.ds(pl.multiple_of(h * half + at, cols), cols)
            total = jnp.zeros((rows, cols), F32)
            for k in range(TAPS):
                lo = (TAPS - 1 - k) * STEP
                total = total + dot_nt(hg[lo : lo + rows, :], w[k, wide, :])
            ga_mine[h, :, pl.ds(at, cols)] = total
            ga_send[h, :, pl.ds(at, cols)] = total.astype(BF16)

        loop(0, half // cols, body)

    def grad_copy(h, i):
        return remote(ga_send.at[h], ga_recv.at[h], "last", i, me, oc)

    activ_grad(oc)
    grad_copy(oc, 0).start()
    activ_grad(c)
    grad_copy(c, 1).start()

    def loss_wait(k):
        loss_copy(k, plane_from(k)).wait_recv()

    loop(1, planes, loss_wait)
    total_loss = jnp.zeros((8, 128), F32)
    for i in range(planes):
        total_loss = total_loss + loss_in[i]
    loss_ref[...] = total_loss[0:1, 0:1] / genes

    for i in range(PIECES):
        to_next(i).wait_send()
        to_prev(i).wait_send()
        left(c, i).wait_send()
        right(c, i).wait_send()
    core(c).wait_send()
    mid.wait_send()

    def z_sent(k):
        gather_a1(track_a1, "track_a1", k, z).wait_send()
        gather_b2(trk_raw, "track_b2", k, z).wait_send()
        pool_b1(k).wait_send()
        pool_a2(k).wait_send()
        gather_a1(grad_a1, "grad_a1", k, z).wait_send()
        gather_b2(grad_b, "grad_b2", k, z).wait_send()

    loop(1, nz, z_sent)

    def plane_sent(k):
        gather_b1(track_b1, "track_b1", k, p).wait_send()
        gather_a2(trk_a, "track_a2", k, p).wait_send()
        pool_a1(0, k).wait_send()
        pool_a1(1, k).wait_send()
        pool_b2(k).wait_send()
        gather_b1(grad_b1, "grad_b1", k, p).wait_send()
        gather_a2(grad_a, "grad_a2", k, p).wait_send()
        loss_copy(k, p).wait_send()

    loop(1, planes, plane_sent)
    grad_copy(c, 0).wait_recv()
    grad_copy(oc, 1).wait_recv()

    def finish(i):
        at = pl.multiple_of(i * ROWS, ROWS)
        some = pl.ds(at, ROWS)
        wide = pl.ds(STEP + at, ROWS)
        v = []
        total = jnp.zeros((ROWS, 1), F32)
        for h in range(2):
            v.append(fac[h, some, :] * (ga_mine[h, some, :] + ga_recv[h, some, :].astype(F32)))
            total = total + jnp.sum(xp[h, wide, :].astype(F32) * v[h], axis=1, keepdims=True)
        own = jnp.where(c == 0, v[0], v[1])
        out_v[some, :] = hg[wide, :].astype(F32) + own - xq[some, :] * total

    loop(0, rows // ROWS, finish)
    grad_copy(oc, 0).wait_send()
    grad_copy(c, 1).wait_send()


def per_device(dims, stop, x, weight, gain, track, start, end, owner, positive):
    ny, nz, nx = dims
    nseq, planes = ny * nz * nx, ny * nx
    rows, half = x.shape
    gl = track.shape[0]
    genes, spans = gl * nseq, start.shape[0]
    group_a, group_b = gl * nz, gl * planes
    padded = rows + 2 * STEP
    cols = half // 3
    wide_a = 2 * cols
    copies = phases(dims)[1]
    dma = pltpu.SemaphoreType.DMA
    vmem = pl.BlockSpec(memory_space=pltpu.VMEM)
    scratch = [
        pltpu.VMEM((2 * half,), F32),
        pltpu.VMEM((gl, half), BF16),
        pltpu.VMEM((1, spans), jnp.int32),
        pltpu.VMEM((1, spans), jnp.int32),
        pltpu.VMEM((1, spans), jnp.int32),
        pltpu.SMEM((gl,), jnp.int32),
        pltpu.VMEM((2, padded, half), BF16),
        pltpu.VMEM((TAPS, 2 * half, half), BF16),
        pltpu.VMEM((2, padded, half), BF16),
        pltpu.VMEM((2, rows, half), F32),
        pltpu.VMEM((rows, half), F32),
        pltpu.VMEM((genes, spans), BF16),
        pltpu.VMEM((padded, spans), BF16),
        pltpu.VMEM((genes, rows), BF16),
        pltpu.VMEM((padded, genes), BF16),
        pltpu.VMEM((genes, rows), BF16),
        pltpu.VMEM((padded, genes), BF16),
        pltpu.VMEM((genes, genes), BF16),
        pltpu.VMEM((genes, genes), BF16),
        pltpu.VMEM((rows, half), F32),
        pltpu.VMEM((rows, half), BF16),
        pltpu.VMEM((2, genes, cols), BF16),
        pltpu.VMEM((2, planes, group_a, cols), BF16),
        pltpu.VMEM((genes, cols), BF16),
        pltpu.VMEM((nz, group_b, cols), BF16),
        pltpu.VMEM((group_a, wide_a), F32),
        pltpu.VMEM((group_b, cols), F32),
        pltpu.VMEM((nz, gl, wide_a), F32),
        pltpu.VMEM((nz, gl, wide_a), F32),
        pltpu.VMEM((planes, gl, cols), F32),
        pltpu.VMEM((planes, gl, cols), F32),
        pltpu.VMEM((nz, gl, wide_a), F32),
        pltpu.VMEM((planes, gl, cols), F32),
        pltpu.VMEM((genes, wide_a), BF16),
        pltpu.VMEM((genes, cols), BF16),
        pltpu.VMEM((genes, cols), BF16),
        pltpu.VMEM((gl, genes + 128), F32),
        pltpu.VMEM((gl, genes + 128), F32),
        pltpu.VMEM((nz, gl, wide_a + 128), F32),
        pltpu.VMEM((planes, gl, cols), F32),
        pltpu.VMEM((genes, wide_a), BF16),
        pltpu.VMEM((genes, cols), BF16),
        pltpu.VMEM((8, 128), F32),
        pltpu.VMEM((planes, 8, 128), F32),
        pltpu.VMEM((padded, half), BF16),
        pltpu.VMEM((2, rows, half), F32),
        pltpu.VMEM((2, rows, half), BF16),
        pltpu.VMEM((2, rows, half), BF16),
        dma((10,)),
        dma((copies,)),
        dma((copies,)),
    ]
    grad, loss = pl.pallas_call(
        functools.partial(kernel, dims, stop),
        out_shape=(
            jax.ShapeDtypeStruct((rows, half), F32),
            jax.ShapeDtypeStruct((1, 1), F32),
        ),
        in_specs=[pl.BlockSpec(memory_space=pltpu.HBM)] * 8,
        out_specs=(vmem, vmem),
        scratch_shapes=scratch,
        compiler_params=pltpu.CompilerParams(
            collective_id=0, has_side_effects=True, vmem_limit_bytes=48 * 1024 * 1024
        ),
    )(
        *(
            pltpu.with_memory_space_constraint(array, pltpu.HBM)
            for array in (
                x,
                weight,
                gain,
                track,
                start.reshape(1, -1),
                end.reshape(1, -1),
                owner.reshape(1, -1),
                positive,
            )
        )
    )
    return grad, loss.reshape(())


def solution(mesh, dims=(4, 8, 4), stop=99):
    return jax.shard_map(
        functools.partial(per_device, dims, stop),
        mesh=mesh,
        in_specs=(
            P("seq", "chan"),
            P(None, None, "chan"),
            P(),
            P("seq", "chan"),
            P(),
            P(),
            P(),
            P("seq"),
        ),
        out_specs=(P("seq", "chan"), P()),
        check_vma=False,
    )
```

time: 1100 us -> 71.1 us (0.06)
  the two profiles are of different devices: /device:TPU:2 before, /device:TPU:1 now
where the time goes in v1:
time: 71.1 us; the launch traced here: 70.1 us
  Pallas kernels  66.9 us (94%)
  between operations  2.33 us (3%)
  local copies, waits for them, and re-layouts  0.88 us (1%)
    pallas_call x1, Pallas kernels, per_device(): pl.pallas_call(functools.partial(kernel, dims, stop), out_shape=(jax.Shap...  66.9 us

profile of v1, /device:TPU:1, one launch (start us, length us, event | category | flops | bytes accessed | tf_op | source)
XLA Modules:
  0.0 70.1 jit_solution(12628428296935072180)
XLA Ops:
  0.6 66.9 %shard_map.95 = (f32[256,768]{1,0:T(8,128)S(1)}, f32[1,1]{1,0:T(1,128)}) custom-call(bf16[256,768]{1,0:T(8,128)(2,1)} %x_hbm.1, bf16[3,1536,768]{2,1,0:T(8,128)(2,1)} %w_hbm.1, f32[1536]{0:T(1024)} %gain_hbm.1, bf16[4,768]{1,0:T(4,128)(2,1)} %track_hbm.1, s32[1,2048]{1,0:T(1,128)} %bitcast.4, s32[1,2048]{1,0:T(1,128)} %bitcast.5, s32[1,2048]{1,0:T(1,128)} %bitcast.6, ...), custom_call_target="tpu_custom_call" | custom-call | tf_op jit(solution)/shard_map/pallas_call | solution.py:724
  67.6 0.9 %copy.12 = f32[256,768]{1,0:T(8,128)} copy(f32[256,768]{1,0:T(8,128)S(1)} %get-tuple-element.8) | data formatting | bytes 1572864

commit v2 on v1

--- a/solution.py
+++ b/solution.py
@@ -57,7 +57,8 @@
         ("left", PIECES),
         ("right", PIECES),
         ("mid", 1),
-        ("last", 2),
+        ("last", 3),
+        ("dots", PIECES),
         ("track_a1", nz),
         ("track_a2", planes),
         ("track_b1", planes),
@@ -140,6 +141,8 @@
     ga_mine,
     ga_send,
     ga_recv,
+    dots,
+    dots_in,
     load_sem,
     send_sem,
     recv_sem,
@@ -191,12 +194,12 @@
     def rows_b(q):
         return pl.ds(pl.multiple_of(q * group_b, group_b), group_b)
 
-    def loop(lo, hi, body):
+    def loop(lo, hi, body, unroll=1):
         def step(i, carry):
             body(i)
             return carry
 
-        lax.fori_loop(lo, hi, step, 0)
+        lax.fori_loop(lo, hi, step, 0, unroll=unroll)
 
     def remote(src, dst, name, k, seq, chan):
         return pltpu.make_async_remote_copy(
@@ -403,12 +406,6 @@
 
     gather_turn(track_a1, track_b1, trk_a, trk_raw, "track")
 
-    tile = min(256, genes)
-
-    def count_rows(i):
-        some = pl.ds(pl.multiple_of(i * tile, tile), tile)
-        counts[some, :] = dot_nt(own_hot[some, :], member[mid_rows, :]).astype(BF16)
-
     keep_left = jnp.where(me > 0, 1.0, 0.0)
     keep_right = jnp.where(me < nseq - 1, 1.0, 0.0)
     for i in range(PIECES):
@@ -417,7 +414,7 @@
         to_prev(i).wait_recv()
         right(c, i).start()
         if i == 0:
-            loop(0, genes // tile, count_rows)
+            counts[...] = dot_nt(own_hot[...], member[mid_rows, :]).astype(BF16)
             loop(0, genes // ROWS, perm_rows)
         else:
             counts_b[...] = dot_nn(perm_t[...], counts[...]).astype(BF16)
@@ -457,11 +454,18 @@
         at = pl.multiple_of(i * ROWS, ROWS)
         some = pl.ds(at, ROWS)
         xs, root = normed_rows(STEP + at)
-        for h in range(2):
-            g = gain_of(h)
-            fac[h, some, :] = gelu_slope(xs[h] * root * g) * (root * g)
-        xq[some, :] = jnp.where(c == 0, xs[0], xs[1]) * (root * root / width)
-
+        mine = jnp.where(c == 0, xs[0], xs[1])
+        g = jnp.where(c == 0, gain_of(0), gain_of(1))
+        fac[some, :] = gelu_slope(mine * root * g) * (root * g)
+        xq[some, :] = mine * (root * root / width)
+
+    tile = min(256, genes)
+    for i in range(genes // tile):
+        some = slice(i * tile, (i + 1) * tile)
+        counts_t[:, some] = dot_nt(member[...], own_hot[some, :]).astype(BF16)
+    for i in range(genes // tile):
+        some = slice(i * tile, (i + 1) * tile)
+        counts_tb[:, some] = dot_nn(counts_t[...], perm[:, some]).astype(BF16)
     loop(0, rows // ROWS, factor_rows)
 
     def pool_b2(k):
@@ -494,12 +498,6 @@
         send_a2[i] = tmp_a[i * gl : (i + 1) * gl, :]
     loop(1, nz, lambda k: pool_a2(k).start())
 
-    def count_cols(i):
-        some = pl.ds(pl.multiple_of(i * STEP, STEP), STEP)
-        counts_t[some, :] = dot_nt(member[some, :], own_hot[...]).astype(BF16)
-        counts_tb[some, :] = dot_nn(counts_t[some, :], perm[...]).astype(BF16)
-
-    loop(0, padded // STEP, count_cols)
     gather_end_a(trk_a, "track")
     gather_end_b(trk_raw, "track")
     trk_b[...] = dot_nn(perm[...], trk_raw[...]).astype(BF16)
@@ -562,49 +560,31 @@
     loop(1, planes, lambda k: loss_copy(k, p).start())
 
     gather_end_b(grad_b, "grad")
-
-    def hidden_grad_b(i):
-        some = pl.ds(pl.multiple_of(i * STEP, STEP), STEP)
-        hg[some, wide_a:half] = dot_nn(counts_tb[some, :], grad_b[...]).astype(BF16)
-
-    loop(0, padded // STEP, hidden_grad_b)
+    hg[:, wide_a:half] = dot_nn(counts_tb[...], grad_b[...]).astype(BF16)
     gather_end_a(grad_a, "grad")
-
-    def hidden_grad_a(i):
-        some = pl.ds(pl.multiple_of(i * STEP, STEP), STEP)
-        hg[some, 0:wide_a] = dot_nn(counts_t[some, :], grad_a[...]).astype(BF16)
-
-    loop(0, padded // STEP, hidden_grad_a)
-
-    def activ_grad(h):
-        def body(i):
-            at = pl.multiple_of(i * cols, cols)
-            wide = pl.ds(pl.multiple_of(h * half + at, cols), cols)
-            total = jnp.zeros((rows, cols), F32)
-            for k in range(TAPS):
-                lo = (TAPS - 1 - k) * STEP
-                total = total + dot_nt(hg[lo : lo + rows, :], w[k, wide, :])
-            ga_mine[h, :, pl.ds(at, cols)] = total
-            ga_send[h, :, pl.ds(at, cols)] = total.astype(BF16)
-
-        loop(0, half // cols, body)
-
-    def grad_copy(h, i):
-        return remote(ga_send.at[h], ga_recv.at[h], "last", i, me, oc)
-
-    activ_grad(oc)
-    grad_copy(oc, 0).start()
-    activ_grad(c)
-    grad_copy(c, 1).start()
+    for i in range(2):
+        some = slice(i * cols, (i + 1) * cols)
+        hg[:, some] = dot_nn(counts_t[...], grad_a[:, some]).astype(BF16)
+
+    def activ_grad(h, i):
+        wide = pl.ds(pl.multiple_of(h * half + i * cols, cols), cols)
+        total = jnp.zeros((rows, cols), F32)
+        for k in range(TAPS):
+            lo = (TAPS - 1 - k) * STEP
+            total = total + dot_nt(hg[lo : lo + rows, :], w[k, wide, :])
+        return total
+
+    def grad_copy(i):
+        return remote(ga_send.at[i], ga_recv.at[i], "last", i, me, oc)
+
+    for i in range(3):
+        ga_send[i] = activ_grad(oc, i).astype(BF16)
+        grad_copy(i).start()
+    for i in range(3):
+        ga_mine[:, i * cols : (i + 1) * cols] = activ_grad(c, i)
 
     def loss_wait(k):
         loss_copy(k, plane_from(k)).wait_recv()
-
-    loop(1, planes, loss_wait)
-    total_loss = jnp.zeros((8, 128), F32)
-    for i in range(planes):
-        total_loss = total_loss + loss_in[i]
-    loss_ref[...] = total_loss[0:1, 0:1] / genes
 
     for i in range(PIECES):
         to_next(i).wait_send()
@@ -635,24 +615,47 @@
         loss_copy(k, p).wait_send()
 
     loop(1, planes, plane_sent)
-    grad_copy(c, 0).wait_recv()
-    grad_copy(oc, 1).wait_recv()
-
-    def finish(i):
-        at = pl.multiple_of(i * ROWS, ROWS)
-        some = pl.ds(at, ROWS)
-        wide = pl.ds(STEP + at, ROWS)
-        v = []
-        total = jnp.zeros((ROWS, 1), F32)
-        for h in range(2):
-            v.append(fac[h, some, :] * (ga_mine[h, some, :] + ga_recv[h, some, :].astype(F32)))
-            total = total + jnp.sum(xp[h, wide, :].astype(F32) * v[h], axis=1, keepdims=True)
-        own = jnp.where(c == 0, v[0], v[1])
-        out_v[some, :] = hg[wide, :].astype(F32) + own - xq[some, :] * total
-
-    loop(0, rows // ROWS, finish)
-    grad_copy(oc, 0).wait_send()
-    grad_copy(c, 1).wait_send()
+    for i in range(3):
+        grad_copy(i).wait_recv()
+    part_rows = rows // PIECES
+
+    def dots_copy(i):
+        return remote(dots.at[i], dots_in.at[i], "dots", i, me, oc)
+
+    for i in range(PIECES):
+
+        def weigh(j):
+            at = pl.multiple_of(j * ROWS, ROWS)
+            some = pl.ds(i * part_rows + at, ROWS)
+            wide = pl.ds(STEP + i * part_rows + at, ROWS)
+            got = jnp.concatenate([ga_recv[n, some, :] for n in range(3)], axis=1)
+            v = fac[some, :] * (ga_mine[some, :] + got.astype(F32))
+            out_v[some, :] = v
+            inner = jnp.sum(xp[c, wide, :].astype(F32) * v, axis=1, keepdims=True)
+            dots[i, pl.ds(at, ROWS), :] = jnp.broadcast_to(inner, (ROWS, 128))
+
+        loop(0, part_rows // ROWS, weigh, unroll=True)
+        dots_copy(i).start()
+    loop(1, planes, loss_wait)
+    total_loss = jnp.zeros((8, 128), F32)
+    for i in range(planes):
+        total_loss = total_loss + loss_in[i]
+    loss_ref[...] = total_loss / genes
+    for i in range(PIECES):
+        dots_copy(i).wait_recv()
+
+        def finish(j):
+            at = pl.multiple_of(j * ROWS, ROWS)
+            some = pl.ds(i * part_rows + at, ROWS)
+            wide = pl.ds(STEP + i * part_rows + at, ROWS)
+            inner = (dots[i, pl.ds(at, ROWS), :] + dots_in[i, pl.ds(at, ROWS), :])[:, 0:1]
+            out_v[some, :] = out_v[some, :] + (hg[wide, :].astype(F32) - xq[some, :] * inner)
+
+        loop(0, part_rows // ROWS, finish, unroll=True)
+    for i in range(3):
+        grad_copy(i).wait_send()
+    for i in range(PIECES):
+        dots_copy(i).wait_send()
 
 
 def per_device(dims, stop, x, weight, gain, track, start, end, owner, positive):
@@ -678,7 +681,7 @@
         pltpu.VMEM((2, padded, half), BF16),
         pltpu.VMEM((TAPS, 2 * half, half), BF16),
         pltpu.VMEM((2, padded, half), BF16),
-        pltpu.VMEM((2, rows, half), F32),
+        pltpu.VMEM((rows, half), F32),
         pltpu.VMEM((rows, half), F32),
         pltpu.VMEM((genes, spans), BF16),
         pltpu.VMEM((padded, spans), BF16),
@@ -714,9 +717,11 @@
         pltpu.VMEM((8, 128), F32),
         pltpu.VMEM((planes, 8, 128), F32),
         pltpu.VMEM((padded, half), BF16),
-        pltpu.VMEM((2, rows, half), F32),
-        pltpu.VMEM((2, rows, half), BF16),
-        pltpu.VMEM((2, rows, half), BF16),
+        pltpu.VMEM((rows, half), F32),
+        pltpu.VMEM((3, rows, cols), BF16),
+        pltpu.VMEM((3, rows, cols), BF16),
+        pltpu.VMEM((PIECES, rows // PIECES, 128), F32),
+        pltpu.VMEM((PIECES, rows // PIECES, 128), F32),
         dma((10,)),
         dma((copies,)),
         dma((copies,)),
@@ -725,7 +730,7 @@
         functools.partial(kernel, dims, stop),
         out_shape=(
             jax.ShapeDtypeStruct((rows, half), F32),
-            jax.ShapeDtypeStruct((1, 1), F32),
+            jax.ShapeDtypeStruct((8, 128), F32),
         ),
         in_specs=[pl.BlockSpec(memory_space=pltpu.HBM)] * 8,
         out_specs=(vmem, vmem),
@@ -748,7 +753,7 @@
             )
         )
     )
-    return grad, loss.reshape(())
+    return grad, loss[0, 0]
 
 
 def solution(mesh, dims=(4, 8, 4), stop=99):

time: 71.1 us -> 68.3 us (0.961)
  Pallas kernels: 66.9 us -> 65.2 us
  between operations: 2.33 us -> 0.64 us
    pallas_call x1, Pallas kernels: 66.9 us -> 65.2 us  [per_device(): pl.pallas_call(functools.partial(kernel, dims, stop), out_shape=(jax.Shap...]
where the time goes in v2:
time: 68.3 us; the launch traced here: 67.2 us
  Pallas kernels  65.2 us (95%)
  local copies, waits for them, and re-layouts  1.39 us (2%)
    pallas_call x1, Pallas kernels, per_device(): pl.pallas_call(functools.partial(kernel, dims, stop), out_shape=(jax.Shap...  65.2 us

profile of v2, /device:TPU:1, one launch (start us, length us, event | category | flops | bytes accessed | tf_op | source)
XLA Modules:
  0.0 67.2 jit_solution(3517862832794022679)
XLA Ops:
  0.6 65.2 %shard_map.95 = (f32[256,768]{1,0:T(8,128)S(1)}, f32[8,128]{1,0:T(8,128)S(1)}) custom-call(bf16[256,768]{1,0:T(8,128)(2,1)} %x_hbm.1, bf16[3,1536,768]{2,1,0:T(8,128)(2,1)} %w_hbm.1, f32[1536]{0:T(1024)} %gain_hbm.1, bf16[4,768]{1,0:T(4,128)(2,1)} %track_hbm.1, s32[1,2048]{1,0:T(1,128)} %bitcast.4, s32[1,2048]{1,0:T(1,128)} %bitcast.5, s32[1,2048]{1,0:T(1,128)} %bitcast.6, ...), custom_call_target="tpu_custom_call" | custom-call | tf_op jit(solution)/shard_map/pallas_call | solution.py:729
  65.8 0.5 slice.3
  66.3 0.9 %copy.11 = f32[256,768]{1,0:T(8,128)} copy(f32[256,768]{1,0:T(8,128)S(1)} %get-tuple-element.8) | data formatting | bytes 1572864

commit v3 on v2

--- a/solution.py
+++ b/solution.py
@@ -17,6 +17,7 @@
 BF16 = jnp.bfloat16
 ROWS = 32
 PIECES = 2
+CHUNKS = 2
 GELU_A = 0.7978845608028654
 GELU_B = 0.044715
 
@@ -31,6 +32,22 @@
     return ((y * nx + x) * nz + z) * genes_each + place
 
 
+def chunk_order(value, dims, genes_each):
+    ny, nz, nx = dims
+    each = genes_each // CHUNKS
+    place = lax.rem(value, genes_each)
+    return lax.div(place, each) * (ny * nz * nx * each) + first_order(
+        lax.div(value, genes_each) * each + lax.rem(place, each), dims, each
+    )
+
+
+def second_from_chunk(row, dims, genes_each):
+    ny, nz, nx = dims
+    each = genes_each // CHUNKS
+    part = ny * nz * nx * each
+    return lax.div(row, part) * part + second_from_first(lax.rem(row, part), dims, each)
+
+
 def second_from_first(row, dims, genes_each):
     ny, nz, nx = dims
     place = lax.rem(row, genes_each)
@@ -47,31 +64,29 @@
     return jnp.dot(a, b, preferred_element_type=F32)
 
 
-def phases(dims):
-    ny, nz, nx = dims
-    planes = ny * nx
+def phases():
     sizes = (
         ("core", 1),
         ("next", PIECES),
         ("prev", PIECES),
         ("left", PIECES),
         ("right", PIECES),
-        ("mid", 1),
+        ("mid", CHUNKS),
         ("last", 3),
         ("dots", PIECES),
-        ("track_a1", nz),
-        ("track_a2", planes),
-        ("track_b1", planes),
-        ("track_b2", nz),
-        ("pool_b1", nz),
-        ("pool_a1", 2 * planes),
-        ("pool_a2", nz),
-        ("pool_b2", planes),
-        ("grad_a1", nz),
-        ("grad_a2", planes),
-        ("grad_b1", planes),
-        ("grad_b2", nz),
-        ("loss", planes),
+        ("track_a1", 1),
+        ("track_a2", 1),
+        ("track_b1", 1),
+        ("track_b2", 1),
+        ("pool_b1", CHUNKS),
+        ("pool_a1", CHUNKS),
+        ("pool_a2", CHUNKS),
+        ("pool_b2", CHUNKS),
+        ("grad_a1", CHUNKS),
+        ("grad_a2", CHUNKS),
+        ("grad_b1", CHUNKS),
+        ("grad_b2", CHUNKS),
+        ("loss", 1),
     )
     at, total = {}, 0
     for name, size in sizes:
@@ -112,6 +127,7 @@
     counts_tb,
     perm,
     perm_t,
+    perm_k,
     acc,
     hid,
     send_a,
@@ -138,6 +154,7 @@
     loss_out,
     loss_in,
     hg,
+    hg_sum,
     ga_mine,
     ga_send,
     ga_recv,
@@ -157,9 +174,13 @@
     genes = gl * nseq
     group_a = gl * nz
     group_b = gl * planes
+    each = gl // CHUNKS
+    part_a = each * nz
+    part_b = each * planes
+    part = each * nseq
     cols = half // 3
     wide_a = 2 * cols
-    first_sem, _ = phases(dims)
+    first_sem, _ = phases()
     me = lax.axis_index("seq")
     c = lax.axis_index("chan")
     oc = 1 - c
@@ -194,6 +215,15 @@
     def rows_b(q):
         return pl.ds(pl.multiple_of(q * group_b, group_b), group_b)
 
+    def chunk_a(n, q):
+        return pl.ds(pl.multiple_of(n * part + q * part_a, part_a), part_a)
+
+    def chunk_b(n, q):
+        return pl.ds(pl.multiple_of(n * part + q * part_b, part_b), part_b)
+
+    def chunk_rows(n):
+        return slice(n * part, (n + 1) * part)
+
     def loop(lo, hi, body, unroll=1):
         def step(i, carry):
             body(i)
@@ -221,6 +251,15 @@
     greet(nxt, c)
     greet(prv, c)
     greet(me, oc)
+
+    def all_in(of, name, k=0):
+        pltpu.make_async_copy(of, of, recv_sem.at[first_sem[name] + k]).wait()
+
+    def all_out(of, name, k=0):
+        pltpu.make_async_copy(of, of, send_sem.at[first_sem[name] + k]).wait()
+
+    others_z = pl.ds(0, nz - 1)
+    others_p = pl.ds(0, planes - 1)
 
     mid_rows = pl.ds(STEP, rows)
     smalls = [
@@ -243,61 +282,61 @@
     for copy in smalls:
         copy.start()
     load_x.start()
+    pl.semaphore_wait(barrier, 3 + planes - 1 + nz - 1)
+
+    piece = STEP // PIECES
+
+    def to_next(i):
+        src = pl.ds(rows - STEP + i * piece, piece)
+        return remote(x_hbm.at[src], xp.at[c, pl.ds(i * piece, piece)], "next", i, nxt, c)
+
+    def to_prev(i):
+        src = pl.ds(i * piece, piece)
+        dst = pl.ds(STEP + rows + i * piece, piece)
+        return remote(x_hbm.at[src], xp.at[c, dst], "prev", i, prv, c)
+
+    def core(side):
+        return remote(x_hbm, xp.at[side, mid_rows], "core", 0, me, oc)
+
+    def left(side, i):
+        some = pl.ds(i * piece, piece)
+        return remote(xp.at[side, some], xp.at[side, some], "left", i, me, oc)
+
+    def right(side, i):
+        some = pl.ds(STEP + rows + i * piece, piece)
+        return remote(xp.at[side, some], xp.at[side, some], "right", i, me, oc)
+
+    core(c).start()
+    to_next(0).start()
+    to_prev(0).start()
+
+    def gather_a1(buf, name, k, slot):
+        return remote(buf.at[z], buf.at[slot], name, 0, z_at(z_to(k)), c)
+
+    def gather_b1(buf, name, k, slot):
+        return remote(buf.at[p], buf.at[slot], name, 0, plane_at(plane_to(k)), c)
+
+    def gather_a2(buf, name, k, q):
+        return remote(buf.at[rows_a(p)], buf.at[rows_a(q)], name, 0, plane_at(plane_to(k)), c)
+
+    def gather_b2(buf, name, k, q):
+        return remote(buf.at[rows_b(z)], buf.at[rows_b(q)], name, 0, z_at(z_to(k)), c)
+
     for copy in smalls:
         copy.wait()
     own_track = track[...].astype(F32)
+    track_b1[p] = own_track[:, wide_a:half]
+    loop(1, planes, lambda k: gather_b1(track_b1, "track_b1", k, p).start())
     track_a1[z] = own_track[:, 0:wide_a]
-    track_b1[p] = own_track[:, wide_a:half]
-    load_x.wait()
-    pl.semaphore_wait(barrier, 3 + planes - 1 + nz - 1)
-
-    piece = STEP // PIECES
-
-    def to_next(i):
-        src = pl.ds(rows + i * piece, piece)
-        return remote(xp.at[c, src], xp.at[c, pl.ds(i * piece, piece)], "next", i, nxt, c)
-
-    def to_prev(i):
-        src = pl.ds(STEP + i * piece, piece)
-        dst = pl.ds(STEP + rows + i * piece, piece)
-        return remote(xp.at[c, src], xp.at[c, dst], "prev", i, prv, c)
-
-    def core(side):
-        return remote(xp.at[side, mid_rows], xp.at[side, mid_rows], "core", 0, me, oc)
-
-    def left(side, i):
-        some = pl.ds(i * piece, piece)
-        return remote(xp.at[side, some], xp.at[side, some], "left", i, me, oc)
-
-    def right(side, i):
-        some = pl.ds(STEP + rows + i * piece, piece)
-        return remote(xp.at[side, some], xp.at[side, some], "right", i, me, oc)
-
-    for i in range(PIECES):
-        to_next(i).start()
-        to_prev(i).start()
-    core(c).start()
-
-    def gather_a1(buf, name, k, slot):
-        return remote(buf.at[z], buf.at[slot], name, k, z_at(z_to(k)), c)
-
-    def gather_b1(buf, name, k, slot):
-        return remote(buf.at[p], buf.at[slot], name, k, plane_at(plane_to(k)), c)
-
-    def gather_a2(buf, name, k, q):
-        return remote(buf.at[rows_a(p)], buf.at[rows_a(q)], name, k, plane_at(plane_to(k)), c)
-
-    def gather_b2(buf, name, k, q):
-        return remote(buf.at[rows_b(z)], buf.at[rows_b(q)], name, k, z_at(z_to(k)), c)
-
     loop(1, nz, lambda k: gather_a1(track_a1, "track_a1", k, z).start())
-    loop(1, planes, lambda k: gather_b1(track_b1, "track_b1", k, p).start())
+    to_next(1).start()
+    to_prev(1).start()
     for copy in load_w:
         copy.start()
 
     first = start[...]
     last = end[...]
-    slot_of = first_order(owner[...], dims, gl)
+    slot_of = chunk_order(owner[...], dims, gl)
     spans = first.shape[1]
     base = me * rows - STEP
 
@@ -316,10 +355,13 @@
         at = pl.multiple_of(i * ROWS, ROWS)
         down = at + lax.broadcasted_iota(jnp.int32, (ROWS, genes), 0)
         across = lax.broadcasted_iota(jnp.int32, (1, genes), 1)
-        moved = second_from_first(at + lax.broadcasted_iota(jnp.int32, (ROWS, 1), 0), dims, gl)
+        row = at + lax.broadcasted_iota(jnp.int32, (ROWS, 1), 0)
         some = pl.ds(at, ROWS)
+        moved = second_from_first(row, dims, gl)
+        perm_k[some, :] = jnp.where(across == moved, 1.0, 0.0).astype(BF16)
+        moved = second_from_chunk(row, dims, gl)
         perm[some, :] = jnp.where(across == moved, 1.0, 0.0).astype(BF16)
-        across = second_from_first(across, dims, gl)
+        across = second_from_chunk(across, dims, gl)
         perm_t[some, :] = jnp.where(across == down, 1.0, 0.0).astype(BF16)
 
     loop(0, genes // ROWS, owner_rows)
@@ -354,6 +396,7 @@
 
         loop(0, count // ROWS, body)
 
+    load_x.wait()
     core(oc).wait_recv()
     activate(STEP, rows, 1.0)
 
@@ -374,35 +417,23 @@
     loop(0, half // cols, centre_cols)
 
     def gather_turn(a1, b1, a2, b2, name):
-        def a_wait(k):
-            gather_a1(a1, name + "_a1", k, z_from(k)).wait_recv()
-
-        loop(1, nz, a_wait)
+        all_in(a1.at[others_z], name + "_a1")
         for i in range(nz):
             tmp_a[i * gl : (i + 1) * gl, :] = a1[i, :, 0:wide_a]
         a2[rows_a(p), :] = tmp_a[...].astype(BF16)
         loop(1, planes, lambda k: gather_a2(a2, name + "_a2", k, p).start())
 
-        def b_wait(k):
-            gather_b1(b1, name + "_b1", k, plane_from(k)).wait_recv()
-
-        loop(1, planes, b_wait)
+        all_in(b1.at[others_p], name + "_b1")
         for i in range(planes):
             tmp_b[i * gl : (i + 1) * gl, :] = b1[i]
         b2[rows_b(z), :] = tmp_b[...].astype(BF16)
         loop(1, nz, lambda k: gather_b2(b2, name + "_b2", k, z).start())
 
     def gather_end_a(a2, name):
-        def a_wait(k):
-            gather_a2(a2, name + "_a2", k, plane_from(k)).wait_recv()
-
-        loop(1, planes, a_wait)
+        all_in(a2.at[pl.ds(0, (planes - 1) * group_a)], name + "_a2")
 
     def gather_end_b(b2, name):
-        def b_wait(k):
-            gather_b2(b2, name + "_b2", k, z_from(k)).wait_recv()
-
-        loop(1, nz, b_wait)
+        all_in(b2.at[pl.ds(0, (nz - 1) * group_b)], name + "_b2")
 
     gather_turn(track_a1, track_b1, trk_a, trk_raw, "track")
 
@@ -427,28 +458,29 @@
         some = slice(i * cols, (i + 1) * cols)
         hid[0:STEP, some] = (acc[0:STEP, some] + tap(0, STEP, 0, some)).astype(BF16)
         hid[STEP:rows, some] = (acc[STEP:rows, some] + tap(STEP + rows, STEP, 2, some)).astype(BF16)
-        return hid[:, some]
-
-    def pool_b1(k):
+
+    def pool_b1(n, k):
         q = z_to(k)
-        return remote(send_b.at[rows_b(q)], recv_b.at[k], "pool_b1", k, z_at(q), c)
-
-    def pool_a1(i, k):
+        return remote(send_b.at[chunk_b(n, q)], recv_b.at[n, k], "pool_b1", n, z_at(q), c)
+
+    def pool_a1(n, k):
         q = plane_to(k)
         return remote(
-            send_a.at[i, rows_a(q)],
-            recv_a.at[i, k],
-            "pool_a1",
-            i * planes + k,
-            plane_at(q),
-            c,
-        )
-
-    send_b[...] = dot_nn(counts_b[...], hidden_cols(2)).astype(BF16)
-    loop(1, nz, lambda k: pool_b1(k).start())
-    for i in range(2):
-        send_a[i] = dot_nn(counts[...], hidden_cols(i)).astype(BF16)
-        loop(1, planes, lambda k: pool_a1(i, k).start())
+            send_a.at[chunk_a(n, q)], recv_a.at[n, k], "pool_a1", n, plane_at(q), c
+        )
+
+    for n in range(CHUNKS):
+        some = chunk_rows(n)
+        for i in range(2):
+            tile = slice(i * cols, (i + 1) * cols)
+            if n == 0:
+                hidden_cols(i)
+            send_a[some, tile] = dot_nn(counts[some, :], hid[:, tile]).astype(BF16)
+        loop(1, planes, lambda k: pool_a1(n, k).start())
+        if n == 0:
+            hidden_cols(2)
+        send_b[some, :] = dot_nn(counts_b[some, :], hid[:, wide_a:half]).astype(BF16)
+        loop(1, nz, lambda k: pool_b1(n, k).start())
 
     def factor_rows(i):
         at = pl.multiple_of(i * ROWS, ROWS)
@@ -468,103 +500,168 @@
         counts_tb[:, some] = dot_nn(counts_t[...], perm[:, some]).astype(BF16)
     loop(0, rows // ROWS, factor_rows)
 
-    def pool_b2(k):
+    def pool_b2(n, k):
         q = plane_to(k)
-        return remote(send_b2.at[q], recv_b2.at[k], "pool_b2", k, plane_at(q), c)
-
-    def pool_a2(k):
+        return remote(
+            send_b2.at[n, q], recv_b2.at[n, k], "pool_b2", n, plane_at(q), c
+        )
+
+    def pool_a2(n, k):
         q = z_to(k)
-        return remote(send_a2.at[q], recv_a2.at[k], "pool_a2", k, z_at(q), c)
-
-    def sum_b1(k, total):
-        pool_b1(k).wait_recv()
-        return total + recv_b[k].astype(F32)
-
-    tmp_b[...] = lax.fori_loop(1, nz, sum_b1, send_b[rows_b(z), :].astype(F32))
-    for i in range(planes):
-        send_b2[i] = tmp_b[i * gl : (i + 1) * gl, :]
-    loop(1, planes, lambda k: pool_b2(k).start())
-
-    for i in range(2):
-
-        def sum_a1(k, total):
-            pool_a1(i, k).wait_recv()
-            return total + recv_a[i, k].astype(F32)
-
-        tmp_a[:, i * cols : (i + 1) * cols] = lax.fori_loop(
-            1, planes, sum_a1, send_a[i, rows_a(p), :].astype(F32)
-        )
-    for i in range(nz):
-        send_a2[i] = tmp_a[i * gl : (i + 1) * gl, :]
-    loop(1, nz, lambda k: pool_a2(k).start())
+        return remote(send_a2.at[n, q], recv_a2.at[n, k], "pool_a2", n, z_at(q), c)
+
+    for n in range(CHUNKS):
+
+        part_sum = send_a[chunk_a(n, p), :].astype(F32)
+        all_in(recv_a.at[n, others_p], "pool_a1", n)
+        for k in range(1, planes):
+            part_sum = part_sum + recv_a[n, k].astype(F32)
+        for i in range(nz):
+            send_a2[n, i] = part_sum[i * each : (i + 1) * each, :]
+        loop(1, nz, lambda k: pool_a2(n, k).start())
+
+        part_sum = send_b[chunk_b(n, z), :].astype(F32)
+        all_in(recv_b.at[n, others_z], "pool_b1", n)
+        for k in range(1, nz):
+            part_sum = part_sum + recv_b[n, k].astype(F32)
+        for i in range(planes):
+            send_b2[n, i] = part_sum[i * each : (i + 1) * each, :]
+        loop(1, planes, lambda k: pool_b2(n, k).start())
 
     gather_end_a(trk_a, "track")
     gather_end_b(trk_raw, "track")
-    trk_b[...] = dot_nn(perm[...], trk_raw[...]).astype(BF16)
-
-    def sum_b2(k, total):
-        pool_b2(k).wait_recv()
-        return total + recv_b2[k]
-
-    mine_b = lax.fori_loop(1, planes, sum_b2, send_b2[p])
-
-    def sum_a2(k, total):
-        pool_a2(k).wait_recv()
-        return total + recv_a2[k]
-
-    mine_a = lax.fori_loop(1, nz, sum_a2, send_a2[z])
-
-    raw_part = dot_nt(mine_a.astype(BF16), trk_a[...]) + dot_nt(mine_b.astype(BF16), trk_b[...])
-    sq_part = jnp.sum(mine_a * mine_a, axis=1, keepdims=True) + jnp.sum(
-        mine_b * mine_b, axis=1, keepdims=True
-    )
-    mid_out[:, 0:genes] = raw_part
-    mid_out[:, genes : genes + 128] = jnp.broadcast_to(sq_part, (gl, 128))
-    mid = remote(mid_out, mid_in, "mid", 0, me, oc)
-    mid.start()
-    mid.wait_recv()
-    both = mid_out[...] + mid_in[...]
-    raw = both[:, 0:genes]
-    scale = lax.rsqrt(both[:, genes : genes + 1] / width + EPS)
-    unit = float(width) ** -0.5
-    logits = raw * (scale * (INV_TEMP * unit))
-    top = jnp.max(logits, axis=1, keepdims=True)
-    log_total = top + jnp.log(jnp.sum(jnp.exp(logits - top), axis=1, keepdims=True))
-    place = lax.broadcasted_iota(jnp.int32, (gl, genes), 0)
-    want = jnp.zeros((gl, genes), jnp.int32)
-    for i in range(gl):
-        want = jnp.where(place == i, first_order(positive[i], dims, gl), want)
-    hits = lax.broadcasted_iota(jnp.int32, (gl, genes), 1) == want
-    weights = jnp.exp(logits - log_total)
-    grad_logit = (LOSS_SCALE * (weights - jnp.where(hits, 1.0, 0.0))).astype(BF16)
-    inner = INV_TEMP * jnp.sum(grad_logit.astype(F32) * raw, axis=1, keepdims=True)
-    back = inner * scale * scale / width
-    outer = unit * scale
-    grad_b1[p] = outer * (INV_TEMP * dot_nn(grad_logit, trk_b[...]) - mine_b * back)
-    loop(1, planes, lambda k: gather_b1(grad_b1, "grad_b1", k, p).start())
-    per_gene = log_total - jnp.sum(jnp.where(hits, logits, 0.0), axis=1, keepdims=True)
-    grad_a1[z, :, 0:wide_a] = outer * (INV_TEMP * dot_nn(grad_logit, trk_a[...]) - mine_a * back)
-    grad_a1[z, :, wide_a : wide_a + 128] = jnp.broadcast_to(per_gene, (gl, 128))
-    loop(1, nz, lambda k: gather_a1(grad_a1, "grad_a1", k, z).start())
-
-    gather_turn(grad_a1, grad_b1, grad_a, grad_b, "grad")
-    part = jnp.zeros((1, 128), F32)
-    for i in range(nz):
-        part = part + jnp.sum(grad_a1[i, :, wide_a : wide_a + 128], axis=0, keepdims=True)
-    loss_out[...] = jnp.broadcast_to(part, (8, 128))
+    trk_b[...] = dot_nn(perm_k[...], trk_raw[...]).astype(BF16)
+
+    def grad_a1_copy(n, k, slot):
+        return remote(
+            grad_a1.at[n, z], grad_a1.at[n, slot], "grad_a1", n, z_at(z_to(k)), c
+        )
+
+    def grad_b1_copy(n, k, slot):
+        return remote(
+            grad_b1.at[n, p],
+            grad_b1.at[n, slot],
+            "grad_b1",
+            n,
+            plane_at(plane_to(k)),
+            c,
+        )
+
+    def grad_a2_copy(n, k, q):
+        return remote(
+            grad_a.at[chunk_a(n, p)],
+            grad_a.at[chunk_a(n, q)],
+            "grad_a2",
+            n,
+            plane_at(plane_to(k)),
+            c,
+        )
+
+    def grad_b2_copy(n, k, q):
+        return remote(
+            grad_b.at[chunk_b(n, z)],
+            grad_b.at[chunk_b(n, q)],
+            "grad_b2",
+            n,
+            z_at(z_to(k)),
+            c,
+        )
+
+    def mid_copy(n):
+        return remote(mid_out.at[n], mid_in.at[n], "mid", n, me, oc)
+
+    for n in range(CHUNKS):
+
+        mine_b = send_b2[n, p]
+        all_in(recv_b2.at[n, others_p], "pool_b2", n)
+        for k in range(1, planes):
+            mine_b = mine_b + recv_b2[n, k]
+        mine_a = send_a2[n, z]
+        all_in(recv_a2.at[n, others_z], "pool_a2", n)
+        for k in range(1, nz):
+            mine_a = mine_a + recv_a2[n, k]
+        raw_part = dot_nt(mine_a.astype(BF16), trk_a[...]) + dot_nt(
+            mine_b.astype(BF16), trk_b[...]
+        )
+        sq_part = jnp.sum(mine_a * mine_a, axis=1, keepdims=True) + jnp.sum(
+            mine_b * mine_b, axis=1, keepdims=True
+        )
+        mid_out[n, :, 0:genes] = raw_part
+        mid_out[n, :, genes : genes + 128] = jnp.broadcast_to(sq_part, (each, 128))
+        mid_copy(n).start()
+        mid_copy(n).wait_recv()
+        both = mid_out[n] + mid_in[n]
+        raw = both[:, 0:genes]
+        scale = lax.rsqrt(both[:, genes : genes + 1] / width + EPS)
+        unit = float(width) ** -0.5
+        logits = raw * (scale * (INV_TEMP * unit))
+        top = jnp.max(logits, axis=1, keepdims=True)
+        log_total = top + jnp.log(jnp.sum(jnp.exp(logits - top), axis=1, keepdims=True))
+        place = lax.broadcasted_iota(jnp.int32, (each, genes), 0)
+        want = jnp.zeros((each, genes), jnp.int32)
+        for i in range(each):
+            want = jnp.where(place == i, first_order(positive[n * each + i], dims, gl), want)
+        hits = lax.broadcasted_iota(jnp.int32, (each, genes), 1) == want
+        weights = jnp.exp(logits - log_total)
+        grad_logit = (LOSS_SCALE * (weights - jnp.where(hits, 1.0, 0.0))).astype(BF16)
+        inner = INV_TEMP * jnp.sum(grad_logit.astype(F32) * raw, axis=1, keepdims=True)
+        back = inner * scale * scale / width
+        outer = unit * scale
+        per_gene = log_total - jnp.sum(jnp.where(hits, logits, 0.0), axis=1, keepdims=True)
+        grad_a1[n, z, :, 0:wide_a] = outer * (
+            INV_TEMP * dot_nn(grad_logit, trk_a[...]) - mine_a * back
+        )
+        grad_a1[n, z, :, wide_a : wide_a + 128] = jnp.broadcast_to(per_gene, (each, 128))
+        loop(1, nz, lambda k: grad_a1_copy(n, k, z).start())
+        grad_b1[n, p] = outer * (INV_TEMP * dot_nn(grad_logit, trk_b[...]) - mine_b * back)
+        loop(1, planes, lambda k: grad_b1_copy(n, k, p).start())
+
+    for n in range(CHUNKS):
+
+        all_in(grad_b1.at[n, others_p], "grad_b1", n)
+        for i in range(planes):
+            tmp_b[i * each : (i + 1) * each, :] = grad_b1[n, i]
+        grad_b[chunk_b(n, z), :] = tmp_b[0:part_b, :].astype(BF16)
+        loop(1, nz, lambda k: grad_b2_copy(n, k, z).start())
+
+        all_in(grad_a1.at[n, others_z], "grad_a1", n)
+        for i in range(nz):
+            tmp_a[i * each : (i + 1) * each, :] = grad_a1[n, i, :, 0:wide_a]
+        grad_a[chunk_a(n, p), :] = tmp_a[0:part_a, :].astype(BF16)
+        loop(1, planes, lambda k: grad_a2_copy(n, k, p).start())
+
+    some_loss = jnp.zeros((1, 128), F32)
+    for n in range(CHUNKS):
+        for i in range(nz):
+            some_loss = some_loss + jnp.sum(
+                grad_a1[n, i, :, wide_a : wide_a + 128], axis=0, keepdims=True
+            )
+    loss_out[...] = jnp.broadcast_to(some_loss, (8, 128))
     loss_in[p] = loss_out[...]
 
     def loss_copy(k, q):
-        return remote(loss_out, loss_in.at[q], "loss", k, plane_at(plane_to(k)), c)
+        return remote(loss_out, loss_in.at[q], "loss", 0, plane_at(plane_to(k)), c)
 
     loop(1, planes, lambda k: loss_copy(k, p).start())
 
-    gather_end_b(grad_b, "grad")
-    hg[:, wide_a:half] = dot_nn(counts_tb[...], grad_b[...]).astype(BF16)
-    gather_end_a(grad_a, "grad")
-    for i in range(2):
-        some = slice(i * cols, (i + 1) * cols)
-        hg[:, some] = dot_nn(counts_t[...], grad_a[:, some]).astype(BF16)
+    for n in range(CHUNKS):
+        some = chunk_rows(n)
+
+        all_in(grad_b.at[pl.ds(0, (nz - 1) * part_b)], "grad_b2", n)
+        for i in (2, 0, 1):
+            tile = slice(i * cols, (i + 1) * cols)
+            if i == 2:
+                total = dot_nn(counts_tb[:, some], grad_b[some, :])
+            else:
+                if i == 0:
+                    all_in(grad_a.at[pl.ds(0, (planes - 1) * part_a)], "grad_a2", n)
+                total = dot_nn(counts_t[:, some], grad_a[some, tile])
+            if n > 0:
+                total = total + hg_sum[:, tile]
+            if n < CHUNKS - 1:
+                hg_sum[:, tile] = total
+            else:
+                hg[:, tile] = total.astype(BF16)
 
     def activ_grad(h, i):
         wide = pl.ds(pl.multiple_of(h * half + i * cols, cols), cols)
@@ -583,38 +680,6 @@
     for i in range(3):
         ga_mine[:, i * cols : (i + 1) * cols] = activ_grad(c, i)
 
-    def loss_wait(k):
-        loss_copy(k, plane_from(k)).wait_recv()
-
-    for i in range(PIECES):
-        to_next(i).wait_send()
-        to_prev(i).wait_send()
-        left(c, i).wait_send()
-        right(c, i).wait_send()
-    core(c).wait_send()
-    mid.wait_send()
-
-    def z_sent(k):
-        gather_a1(track_a1, "track_a1", k, z).wait_send()
-        gather_b2(trk_raw, "track_b2", k, z).wait_send()
-        pool_b1(k).wait_send()
-        pool_a2(k).wait_send()
-        gather_a1(grad_a1, "grad_a1", k, z).wait_send()
-        gather_b2(grad_b, "grad_b2", k, z).wait_send()
-
-    loop(1, nz, z_sent)
-
-    def plane_sent(k):
-        gather_b1(track_b1, "track_b1", k, p).wait_send()
-        gather_a2(trk_a, "track_a2", k, p).wait_send()
-        pool_a1(0, k).wait_send()
-        pool_a1(1, k).wait_send()
-        pool_b2(k).wait_send()
-        gather_b1(grad_b1, "grad_b1", k, p).wait_send()
-        gather_a2(grad_a, "grad_a2", k, p).wait_send()
-        loss_copy(k, p).wait_send()
-
-    loop(1, planes, plane_sent)
     for i in range(3):
         grad_copy(i).wait_recv()
     part_rows = rows // PIECES
@@ -636,7 +701,7 @@
 
         loop(0, part_rows // ROWS, weigh, unroll=True)
         dots_copy(i).start()
-    loop(1, planes, loss_wait)
+    all_in(loss_in.at[others_p], "loss")
     total_loss = jnp.zeros((8, 128), F32)
     for i in range(planes):
         total_loss = total_loss + loss_in[i]
@@ -652,6 +717,29 @@
             out_v[some, :] = out_v[some, :] + (hg[wide, :].astype(F32) - xq[some, :] * inner)
 
         loop(0, part_rows // ROWS, finish, unroll=True)
+    for i in range(PIECES):
+        to_next(i).wait_send()
+        to_prev(i).wait_send()
+        left(c, i).wait_send()
+        right(c, i).wait_send()
+    core(c).wait_send()
+
+    all_out(track_a1.at[others_z], "track_a1")
+    all_out(track_b1.at[others_p], "track_b1")
+    all_out(trk_a.at[pl.ds(0, (planes - 1) * group_a)], "track_a2")
+    all_out(trk_raw.at[pl.ds(0, (nz - 1) * group_b)], "track_b2")
+    all_out(loss_in.at[others_p], "loss")
+    for n in range(CHUNKS):
+        all_out(recv_a.at[n, others_p], "pool_a1", n)
+        all_out(recv_b.at[n, others_z], "pool_b1", n)
+        all_out(recv_a2.at[n, others_z], "pool_a2", n)
+        all_out(recv_b2.at[n, others_p], "pool_b2", n)
+        all_out(grad_a1.at[n, others_z], "grad_a1", n)
+        all_out(grad_b1.at[n, others_p], "grad_b1", n)
+        all_out(grad_a.at[pl.ds(0, (planes - 1) * part_a)], "grad_a2", n)
+        all_out(grad_b.at[pl.ds(0, (nz - 1) * part_b)], "grad_b2", n)
+    for n in range(CHUNKS):
+        mid_copy(n).wait_send()
     for i in range(3):
         grad_copy(i).wait_send()
     for i in range(PIECES):
@@ -666,9 +754,10 @@
     genes, spans = gl * nseq, start.shape[0]
     group_a, group_b = gl * nz, gl * planes
     padded = rows + 2 * STEP
+    each = gl // CHUNKS
     cols = half // 3
     wide_a = 2 * cols
-    copies = phases(dims)[1]
+    copies = phases()[1]
     dma = pltpu.SemaphoreType.DMA
     vmem = pl.BlockSpec(memory_space=pltpu.VMEM)
     scratch = [
@@ -691,32 +780,34 @@
         pltpu.VMEM((padded, genes), BF16),
         pltpu.VMEM((genes, genes), BF16),
         pltpu.VMEM((genes, genes), BF16),
+        pltpu.VMEM((genes, genes), BF16),
         pltpu.VMEM((rows, half), F32),
         pltpu.VMEM((rows, half), BF16),
-        pltpu.VMEM((2, genes, cols), BF16),
-        pltpu.VMEM((2, planes, group_a, cols), BF16),
+        pltpu.VMEM((genes, wide_a), BF16),
+        pltpu.VMEM((CHUNKS, planes, each * nz, wide_a), BF16),
         pltpu.VMEM((genes, cols), BF16),
-        pltpu.VMEM((nz, group_b, cols), BF16),
+        pltpu.VMEM((CHUNKS, nz, each * planes, cols), BF16),
         pltpu.VMEM((group_a, wide_a), F32),
         pltpu.VMEM((group_b, cols), F32),
-        pltpu.VMEM((nz, gl, wide_a), F32),
-        pltpu.VMEM((nz, gl, wide_a), F32),
-        pltpu.VMEM((planes, gl, cols), F32),
-        pltpu.VMEM((planes, gl, cols), F32),
+        pltpu.VMEM((CHUNKS, nz, each, wide_a), F32),
+        pltpu.VMEM((CHUNKS, nz, each, wide_a), F32),
+        pltpu.VMEM((CHUNKS, planes, each, cols), F32),
+        pltpu.VMEM((CHUNKS, planes, each, cols), F32),
         pltpu.VMEM((nz, gl, wide_a), F32),
         pltpu.VMEM((planes, gl, cols), F32),
         pltpu.VMEM((genes, wide_a), BF16),
         pltpu.VMEM((genes, cols), BF16),
         pltpu.VMEM((genes, cols), BF16),
-        pltpu.VMEM((gl, genes + 128), F32),
-        pltpu.VMEM((gl, genes + 128), F32),
-        pltpu.VMEM((nz, gl, wide_a + 128), F32),
-        pltpu.VMEM((planes, gl, cols), F32),
+        pltpu.VMEM((CHUNKS, each, genes + 128), F32),
+        pltpu.VMEM((CHUNKS, each, genes + 128), F32),
+        pltpu.VMEM((CHUNKS, nz, each, wide_a + 128), F32),
+        pltpu.VMEM((CHUNKS, planes, each, cols), F32),
         pltpu.VMEM((genes, wide_a), BF16),
         pltpu.VMEM((genes, cols), BF16),
         pltpu.VMEM((8, 128), F32),
         pltpu.VMEM((planes, 8, 128), F32),
         pltpu.VMEM((padded, half), BF16),
+        pltpu.VMEM((padded, half), F32),
         pltpu.VMEM((rows, half), F32),
         pltpu.VMEM((3, rows, cols), BF16),
         pltpu.VMEM((3, rows, cols), BF16),

time: 68.3 us -> 61.6 us (0.902); the launches traced: 67.2 us -> 61.6 us
  Pallas kernels: 65.2 us -> 59.5 us
    pallas_call x1, Pallas kernels: 65.2 us -> 59.5 us  [per_device(): pl.pallas_call(functools.partial(kernel, dims, stop), out_shape=(jax.Shap...]
where the time goes in v3:
time: 61.6 us
  Pallas kernels  59.5 us (97%)
  local copies, waits for them, and re-layouts  1.39 us (2%)
  between operations  0.64 us (1%)
    pallas_call x1, Pallas kernels, per_device(): pl.pallas_call(functools.partial(kernel, dims, stop), out_shape=(jax.Shap...  59.5 us

profile of v3, /device:TPU:1, one launch (start us, length us, event | category | flops | bytes accessed | tf_op | source)
XLA Modules:
  0.0 61.6 jit_solution(16288826118794108764)
XLA Ops:
  0.6 59.5 %shard_map.95 = (f32[256,768]{1,0:T(8,128)S(1)}, f32[8,128]{1,0:T(8,128)S(1)}) custom-call(bf16[256,768]{1,0:T(8,128)(2,1)} %x_hbm.1, bf16[3,1536,768]{2,1,0:T(8,128)(2,1)} %w_hbm.1, f32[1536]{0:T(1024)} %gain_hbm.1, bf16[4,768]{1,0:T(4,128)(2,1)} %track_hbm.1, s32[1,2048]{1,0:T(1,128)} %bitcast.4, s32[1,2048]{1,0:T(1,128)} %bitcast.5, s32[1,2048]{1,0:T(1,128)} %bitcast.6, ...), custom_call_target="tpu_custom_call" | custom-call | tf_op jit(solution)/shard_map/pallas_call | solution.py:820
  60.2 0.5 slice.3
  60.7 0.9 %copy.11 = f32[256,768]{1,0:T(8,128)} copy(f32[256,768]{1,0:T(8,128)S(1)} %get-tuple-element.8) | data formatting | bytes 1572864

commit v4 on v3

--- a/solution.py
+++ b/solution.py
@@ -209,6 +209,11 @@
     def z_from(k):
         return lax.rem(z + nz - k, nz)
 
+    plane_q = [plane_to(k) for k in range(planes)]
+    plane_id = [plane_at(q) for q in plane_q]
+    z_q = [z_to(k) for k in range(nz)]
+    z_id = [z_at(q) for q in z_q]
+
     def rows_a(q):
         return pl.ds(pl.multiple_of(q * group_a, group_a), group_a)
 
@@ -246,8 +251,10 @@
     def greet(seq, chan):
         pl.semaphore_signal(barrier, inc=1, device_id=(seq, chan), device_id_type=MESH)
 
-    loop(1, nz, lambda k: greet(z_at(z_to(k)), c))
-    loop(1, planes, lambda k: greet(plane_at(plane_to(k)), c))
+    for k in range(1, nz):
+        greet(z_id[k], c)
+    for k in range(1, planes):
+        greet(plane_id[k], c)
     greet(nxt, c)
     greet(prv, c)
     greet(me, oc)
@@ -311,24 +318,26 @@
     to_prev(0).start()
 
     def gather_a1(buf, name, k, slot):
-        return remote(buf.at[z], buf.at[slot], name, 0, z_at(z_to(k)), c)
+        return remote(buf.at[z], buf.at[slot], name, 0, z_id[k], c)
 
     def gather_b1(buf, name, k, slot):
-        return remote(buf.at[p], buf.at[slot], name, 0, plane_at(plane_to(k)), c)
+        return remote(buf.at[p], buf.at[slot], name, 0, plane_id[k], c)
 
     def gather_a2(buf, name, k, q):
-        return remote(buf.at[rows_a(p)], buf.at[rows_a(q)], name, 0, plane_at(plane_to(k)), c)
+        return remote(buf.at[rows_a(p)], buf.at[rows_a(q)], name, 0, plane_id[k], c)
 
     def gather_b2(buf, name, k, q):
-        return remote(buf.at[rows_b(z)], buf.at[rows_b(q)], name, 0, z_at(z_to(k)), c)
+        return remote(buf.at[rows_b(z)], buf.at[rows_b(q)], name, 0, z_id[k], c)
 
     for copy in smalls:
         copy.wait()
     own_track = track[...].astype(F32)
     track_b1[p] = own_track[:, wide_a:half]
-    loop(1, planes, lambda k: gather_b1(track_b1, "track_b1", k, p).start())
+    for k in range(1, planes):
+        gather_b1(track_b1, "track_b1", k, p).start()
     track_a1[z] = own_track[:, 0:wide_a]
-    loop(1, nz, lambda k: gather_a1(track_a1, "track_a1", k, z).start())
+    for k in range(1, nz):
+        gather_a1(track_a1, "track_a1", k, z).start()
     to_next(1).start()
     to_prev(1).start()
     for copy in load_w:
@@ -421,13 +430,15 @@
         for i in range(nz):
             tmp_a[i * gl : (i + 1) * gl, :] = a1[i, :, 0:wide_a]
         a2[rows_a(p), :] = tmp_a[...].astype(BF16)
-        loop(1, planes, lambda k: gather_a2(a2, name + "_a2", k, p).start())
+        for k in range(1, planes):
+            gather_a2(a2, name + "_a2", k, p).start()
 
         all_in(b1.at[others_p], name + "_b1")
         for i in range(planes):
             tmp_b[i * gl : (i + 1) * gl, :] = b1[i]
         b2[rows_b(z), :] = tmp_b[...].astype(BF16)
-        loop(1, nz, lambda k: gather_b2(b2, name + "_b2", k, z).start())
+        for k in range(1, nz):
+            gather_b2(b2, name + "_b2", k, z).start()
 
     def gather_end_a(a2, name):
         all_in(a2.at[pl.ds(0, (planes - 1) * group_a)], name + "_a2")
@@ -460,13 +471,13 @@
         hid[STEP:rows, some] = (acc[STEP:rows, some] + tap(STEP + rows, STEP, 2, some)).astype(BF16)
 
     def pool_b1(n, k):
-        q = z_to(k)
-        return remote(send_b.at[chunk_b(n, q)], recv_b.at[n, k], "pool_b1", n, z_at(q), c)
+        q = z_q[k]
+        return remote(send_b.at[chunk_b(n, q)], recv_b.at[n, k], "pool_b1", n, z_id[k], c)
 
     def pool_a1(n, k):
-        q = plane_to(k)
+        q = plane_q[k]
         return remote(
-            send_a.at[chunk_a(n, q)], recv_a.at[n, k], "pool_a1", n, plane_at(q), c
+            send_a.at[chunk_a(n, q)], recv_a.at[n, k], "pool_a1", n, plane_id[k], c
         )
 
     for n in range(CHUNKS):
@@ -476,11 +487,13 @@
             if n == 0:
                 hidden_cols(i)
             send_a[some, tile] = dot_nn(counts[some, :], hid[:, tile]).astype(BF16)
-        loop(1, planes, lambda k: pool_a1(n, k).start())
+        for k in range(1, planes):
+            pool_a1(n, k).start()
         if n == 0:
             hidden_cols(2)
         send_b[some, :] = dot_nn(counts_b[some, :], hid[:, wide_a:half]).astype(BF16)
-        loop(1, nz, lambda k: pool_b1(n, k).start())
+        for k in range(1, nz):
+            pool_b1(n, k).start()
 
     def factor_rows(i):
         at = pl.multiple_of(i * ROWS, ROWS)
@@ -498,17 +511,16 @@
     for i in range(genes // tile):
         some = slice(i * tile, (i + 1) * tile)
         counts_tb[:, some] = dot_nn(counts_t[...], perm[:, some]).astype(BF16)
-    loop(0, rows // ROWS, factor_rows)
 
     def pool_b2(n, k):
-        q = plane_to(k)
+        q = plane_q[k]
         return remote(
-            send_b2.at[n, q], recv_b2.at[n, k], "pool_b2", n, plane_at(q), c
+            send_b2.at[n, q], recv_b2.at[n, k], "pool_b2", n, plane_id[k], c
         )
 
     def pool_a2(n, k):
-        q = z_to(k)
-        return remote(send_a2.at[n, q], recv_a2.at[n, k], "pool_a2", n, z_at(q), c)
+        q = z_q[k]
+        return remote(send_a2.at[n, q], recv_a2.at[n, k], "pool_a2", n, z_id[k], c)
 
     for n in range(CHUNKS):
 
@@ -518,7 +530,8 @@
             part_sum = part_sum + recv_a[n, k].astype(F32)
         for i in range(nz):
             send_a2[n, i] = part_sum[i * each : (i + 1) * each, :]
-        loop(1, nz, lambda k: pool_a2(n, k).start())
+        for k in range(1, nz):
+            pool_a2(n, k).start()
 
         part_sum = send_b[chunk_b(n, z), :].astype(F32)
         all_in(recv_b.at[n, others_z], "pool_b1", n)
@@ -526,7 +539,8 @@
             part_sum = part_sum + recv_b[n, k].astype(F32)
         for i in range(planes):
             send_b2[n, i] = part_sum[i * each : (i + 1) * each, :]
-        loop(1, planes, lambda k: pool_b2(n, k).start())
+        for k in range(1, planes):
+            pool_b2(n, k).start()
 
     gather_end_a(trk_a, "track")
     gather_end_b(trk_raw, "track")
@@ -534,7 +548,7 @@
 
     def grad_a1_copy(n, k, slot):
         return remote(
-            grad_a1.at[n, z], grad_a1.at[n, slot], "grad_a1", n, z_at(z_to(k)), c
+            grad_a1.at[n, z], grad_a1.at[n, slot], "grad_a1", n, z_id[k], c
         )
 
     def grad_b1_copy(n, k, slot):
@@ -543,7 +557,7 @@
             grad_b1.at[n, slot],
             "grad_b1",
             n,
-            plane_at(plane_to(k)),
+            plane_id[k],
             c,
         )
 
@@ -553,7 +567,7 @@
             grad_a.at[chunk_a(n, q)],
             "grad_a2",
             n,
-            plane_at(plane_to(k)),
+            plane_id[k],
             c,
         )
 
@@ -563,7 +577,7 @@
             grad_b.at[chunk_b(n, q)],
             "grad_b2",
             n,
-            z_at(z_to(k)),
+            z_id[k],
             c,
         )
 
@@ -612,9 +626,11 @@
             INV_TEMP * dot_nn(grad_logit, trk_a[...]) - mine_a * back
         )
         grad_a1[n, z, :, wide_a : wide_a + 128] = jnp.broadcast_to(per_gene, (each, 128))
-        loop(1, nz, lambda k: grad_a1_copy(n, k, z).start())
+        for k in range(1, nz):
+            grad_a1_copy(n, k, z).start()
         grad_b1[n, p] = outer * (INV_TEMP * dot_nn(grad_logit, trk_b[...]) - mine_b * back)
-        loop(1, planes, lambda k: grad_b1_copy(n, k, p).start())
+        for k in range(1, planes):
+            grad_b1_copy(n, k, p).start()
 
     for n in range(CHUNKS):
 
@@ -622,13 +638,15 @@
         for i in range(planes):
             tmp_b[i * each : (i + 1) * each, :] = grad_b1[n, i]
         grad_b[chunk_b(n, z), :] = tmp_b[0:part_b, :].astype(BF16)
-        loop(1, nz, lambda k: grad_b2_copy(n, k, z).start())
+        for k in range(1, nz):
+            grad_b2_copy(n, k, z).start()
 
         all_in(grad_a1.at[n, others_z], "grad_a1", n)
         for i in range(nz):
             tmp_a[i * each : (i + 1) * each, :] = grad_a1[n, i, :, 0:wide_a]
         grad_a[chunk_a(n, p), :] = tmp_a[0:part_a, :].astype(BF16)
-        loop(1, planes, lambda k: grad_a2_copy(n, k, p).start())
+        for k in range(1, planes):
+            grad_a2_copy(n, k, p).start()
 
     some_loss = jnp.zeros((1, 128), F32)
     for n in range(CHUNKS):
@@ -640,9 +658,12 @@
     loss_in[p] = loss_out[...]
 
     def loss_copy(k, q):
-        return remote(loss_out, loss_in.at[q], "loss", 0, plane_at(plane_to(k)), c)
-
-    loop(1, planes, lambda k: loss_copy(k, p).start())
+        return remote(loss_out, loss_in.at[q], "loss", 0, plane_id[k], c)
+
+    for k in range(1, planes):
+        loss_copy(k, p).start()
+
+    loop(0, rows // ROWS, factor_rows)
 
     for n in range(CHUNKS):
         some = chunk_rows(n)

time: 61.6 us -> 60.4 us (0.981)
  Pallas kernels: 59.5 us -> 58.3 us
    pallas_call x1, Pallas kernels: 59.5 us -> 58.3 us  [per_device(): pl.pallas_call(functools.partial(kernel, dims, stop), out_shape=(jax.Shap...]
where the time goes in v4:
time: 60.4 us; the launch traced here: 60.3 us
  Pallas kernels  58.3 us (97%)
  local copies, waits for them, and re-layouts  1.39 us (2%)
  between operations  0.64 us (1%)
    pallas_call x1, Pallas kernels, per_device(): pl.pallas_call(functools.partial(kernel, dims, stop), out_shape=(jax.Shap...  58.3 us

profile of v4, /device:TPU:1, one launch (start us, length us, event | category | flops | bytes accessed | tf_op | source)
XLA Modules:
  0.0 60.3 jit_solution(1067002305203376552)
XLA Ops:
  0.6 58.3 %shard_map.95 = (f32[256,768]{1,0:T(8,128)S(1)}, f32[8,128]{1,0:T(8,128)S(1)}) custom-call(bf16[256,768]{1,0:T(8,128)(2,1)} %x_hbm.1, bf16[3,1536,768]{2,1,0:T(8,128)(2,1)} %w_hbm.1, f32[1536]{0:T(1024)} %gain_hbm.1, bf16[4,768]{1,0:T(4,128)(2,1)} %track_hbm.1, s32[1,2048]{1,0:T(1,128)} %bitcast.4, s32[1,2048]{1,0:T(1,128)} %bitcast.5, s32[1,2048]{1,0:T(1,128)} %bitcast.6, ...), custom_call_target="tpu_custom_call" | custom-call | tf_op jit(solution)/shard_map/pallas_call | solution.py:841
  58.9 0.5 slice.3
  59.4 0.9 %copy.11 = f32[256,768]{1,0:T(8,128)} copy(f32[256,768]{1,0:T(8,128)S(1)} %get-tuple-element.8) | data formatting | bytes 1572864
